TPU v7x, 256 devices: a whole 4x4x8 slice. The times are simulated.
256 devices in a mesh: queue: 32 (over x, y, core), seq: 8 (over z).
Axes of the slice: x: 4, y: 4, z: 8, core: 2. Of those that a mesh axis runs over, the one named last changes fastest.
Arguments:
- hidden: bfloat16 [256, 64, 3072], P('seq', 'queue'), may hold values from -6 to 6
- latent: bfloat16 [256, 64, 64], P('seq', 'queue'), may hold values from -6 to 6
- fresh_noise: bfloat16 [256, 64], P('seq'), may hold values from -6 to 6
- timesteps: int32 [64], P('queue'), may hold values from 16 to 1039, as said below
- queue_slots: int32 [64], replicated, may hold values from 0 to 127, as said below
- windows: int32 [64], replicated, may hold values from 1 to 2, as said below
- mod_weight: bfloat16 [3, 128, 3072], P(None, None, 'seq'), may hold values from -0.5 to 0.5
- attention_weight: bfloat16 [3072, 12288], P(None, 'seq')
- final_weight: bfloat16 [3072, 64], replicated, may hold values from -0.109375 to 0.109375
Outputs:
- block_out: bfloat16 [256, 64, 3072], P('seq', 'queue')
- noise_pred: bfloat16 [256, 64, 64], P('seq', 'queue')
- new_queue: bfloat16 [256, 64, 64], P('seq', 'queue')
Inputs may be any that keep to these rules, and one draw needn't show every extreme that they name: `timesteps`: frame f has a timestep from (f + 1) * 16 to (f + 2) * 16 - 1. `queue_slots`: frame f has the slot 2 f or 2 f + 1; the first frame has slot 0 and the last the slot 127. `windows`: some frame has a window of 2.
All inputs are finite; a program needn't handle non-finite values.
Results may differ from a plain program's by a relative error of at most 0.02.
Values may be sent and summed in bfloat16 or wider, within the bound.
A program may use at most 128 MiB of HBM per device.

v0:
```python
import math

import jax
import jax.numpy as jnp
from jax import lax
from jax.sharding import PartitionSpec as P

HD = 128
STRIDE = 16
WMAX = 2


LN_EPS = 1e-06
DECAY = 2.3
NEAR_COST = 0.5


def shifted(value, axis, steps):
    count = lax.axis_size(axis)
    leading, last = (max(0, -steps), min(count, count - steps))
    return lax.ppermute(value, axis, [(source, source + steps) for source in range(leading, last)])


def frequencies(timestep_ids, embed_width):
    half_width = embed_width // 2
    ladder = jnp.exp(jnp.arange(half_width, dtype=jnp.float32) * (-math.log(10000.0) / half_width))
    angles = timestep_ids.astype(jnp.float32)[:, None] * ladder[None, :]
    return jnp.concatenate([jnp.cos(angles), jnp.sin(angles)], axis=1)


def plan(timestep_ids, horizon):
    return jnp.exp(timestep_ids.astype(jnp.float32) * (-DECAY / horizon))


def denoise(latent_now, noise_term, timestep_ids, horizon):
    alpha_now = plan(timestep_ids, horizon)
    before = plan(timestep_ids - STRIDE, horizon)
    clean_part = (latent_now - jnp.sqrt(1.0 - alpha_now) * noise_term) / jnp.sqrt(alpha_now)
    return jnp.sqrt(before) * clean_part + jnp.sqrt(1.0 - before) * noise_term


def spatial(queries, key_rows, value_rows):
    factor = 1.0 / math.sqrt(queries.shape[-1])
    scores = (
        jnp.einsum("qhe,khe->hqk", queries, key_rows, preferred_element_type=jnp.float32) * factor
    )
    peak = jnp.max(scores, axis=2, keepdims=True)
    expo_terms = jnp.exp(scores - peak)
    denominator = jnp.sum(expo_terms, axis=2)
    combined = jnp.einsum(
        "hqk,khe->qhe",
        expo_terms.astype(jnp.bfloat16),
        value_rows,
        preferred_element_type=jnp.float32,
    )
    return combined / jnp.transpose(denominator)[:, :, None]


def temporal(queries, keys_pad, values_pad, queue_slots, windows):
    frames_here = queries.shape[1]
    reach_span = 2 * WMAX + 1
    frame_total = queue_slots.shape[0]
    factor = 1.0 / math.sqrt(queries.shape[-1])
    near_keys = jnp.stack(
        [keys_pad[:, offset : offset + frames_here] for offset in range(reach_span)], axis=2
    )
    near_values = jnp.stack(
        [values_pad[:, offset : offset + frames_here] for offset in range(reach_span)], axis=2
    )
    scores = (
        jnp.einsum("rihe,ridhe->ridh", queries, near_keys, preferred_element_type=jnp.float32)
        * factor
    )
    padded_slots = jnp.pad(queue_slots, (WMAX, WMAX))
    near_slots = jnp.stack(
        [padded_slots[offset : offset + frames_here] for offset in range(reach_span)], axis=1
    )
    frame_index = (
        jnp.arange(frames_here, dtype=jnp.int32)[:, None]
        + jnp.arange(reach_span, dtype=jnp.int32)[None, :]
        - WMAX
    )
    slot_gap = jnp.abs(near_slots - queue_slots[:, None])
    allowed = (frame_index >= 0) & (frame_index < frame_total) & (slot_gap <= windows[:, None])
    logits = scores - NEAR_COST * slot_gap.astype(jnp.float32)[None, :, :, None]
    inside = allowed[None, :, :, None]
    peak = jnp.max(jnp.where(inside, logits, -1e30), axis=2, keepdims=True)
    weights = jnp.where(inside, jnp.exp(jnp.where(inside, logits, peak) - peak), 0.0)
    summed = jnp.sum(weights, axis=2)
    combined = jnp.einsum("ridh,ridhe->rihe", weights, near_values.astype(jnp.float32))
    return combined / summed[..., None]


def shards(
    hidden,
    latent,
    fresh_noise,
    timesteps,
    queue_slots,
    windows,
    mod_weight,
    attention_weight,
    final_weight,
):
    tokens_here, frames_here, features = hidden.shape
    queue_count = lax.axis_size("queue")
    seq_count = lax.axis_size("seq")
    queue_place = lax.axis_index("queue")
    frame_tokens = tokens_here * seq_count
    frame_total = frames_here * queue_count
    horizon = STRIDE * (frame_total + 1)
    local_heads = attention_weight.shape[1] // (4 * HD)
    embedded = jax.nn.silu(frequencies(timesteps, mod_weight.shape[1])).astype(jnp.bfloat16)
    mod_part = jnp.einsum("fk,pkd->pfd", embedded, mod_weight, preferred_element_type=jnp.float32)
    modulation = lax.all_gather(mod_part, "seq", axis=2, tiled=True)
    values = hidden.astype(jnp.float32)
    centred = values - jnp.mean(values, axis=2, keepdims=True)
    variance = jnp.mean(centred * centred, axis=2, keepdims=True)
    normal = (
        centred * lax.rsqrt(variance + LN_EPS) * (1.0 + modulation[1][None]) + modulation[0][None]
    ).astype(jnp.bfloat16)
    layout = attention_weight.reshape(features, local_heads, 4, HD)
    qkv_weight = layout[:, :, :3, :].reshape(features, local_heads * 3 * HD)
    out_weight = layout[:, :, 3, :].reshape(features, local_heads * HD)
    product = jnp.einsum(
        "tfd,de->tfe",
        lax.all_gather(normal, "seq", axis=0, tiled=True),
        qkv_weight,
        preferred_element_type=jnp.float32,
    )
    projected = product.astype(jnp.bfloat16)
    projected = projected.reshape(frame_tokens, frames_here, local_heads, 3, HD)
    queries = projected[:, :, :, 0]
    key_rows = projected[:, :, :, 1]
    value_rows = projected[:, :, :, 2]
    block_rows = math.gcd(frame_tokens, 512)

    def frame_attend(triple):
        frame_queries, frame_keys, frame_values = triple
        grouped = frame_queries.reshape(frame_tokens // block_rows, block_rows, local_heads, HD)

        def one_block(query_block):
            return spatial(query_block, frame_keys, frame_values)

        result = lax.map(one_block, grouped)
        return result.reshape(frame_tokens, local_heads, HD)

    spread = lax.map(
        frame_attend,
        (jnp.moveaxis(queries, 1, 0), jnp.moveaxis(key_rows, 1, 0), jnp.moveaxis(value_rows, 1, 0)),
    )
    spread = jnp.moveaxis(spread, 0, 1)
    sub_queries = lax.all_to_all(queries, "queue", split_axis=0, concat_axis=1, tiled=True)
    sub_keys = lax.all_to_all(key_rows, "queue", split_axis=0, concat_axis=1, tiled=True)
    sub_values = lax.all_to_all(value_rows, "queue", split_axis=0, concat_axis=1, tiled=True)
    edge = ((0, 0), (WMAX, WMAX), (0, 0), (0, 0))
    result = temporal(
        sub_queries, jnp.pad(sub_keys, edge), jnp.pad(sub_values, edge), queue_slots, windows
    )
    along = lax.all_to_all(
        result.astype(jnp.bfloat16), "queue", split_axis=1, concat_axis=0, tiled=True
    ).astype(result.dtype)
    heads = (
        (spread + along).astype(jnp.bfloat16).reshape(frame_tokens, frames_here, local_heads * HD)
    )
    head_rows = heads.reshape(frame_tokens * frames_here, local_heads * HD)
    combined = lax.psum_scatter(
        lax.dot_general(
            head_rows, out_weight, (((1,), (1,)), ((), ())), preferred_element_type=jnp.float32
        ).astype(jnp.bfloat16),
        "seq",
        scatter_dimension=0,
        tiled=True,
    ).astype(jnp.float32)
    combined = combined.reshape(tokens_here, frames_here, features)
    block_out = (values + modulation[2][None] * combined).astype(jnp.bfloat16)
    noise_term = jnp.einsum(
        "tfd,dc->tfc", block_out, final_weight, preferred_element_type=jnp.float32
    )
    noise_pred = noise_term.astype(jnp.bfloat16)
    updated = denoise(latent.astype(jnp.float32), noise_term, timesteps[:, None], horizon).astype(
        jnp.bfloat16
    )
    arriving = shifted(updated[:, 0], "queue", -1)
    arriving = jnp.where(queue_place == queue_count - 1, fresh_noise, arriving)
    new_queue = jnp.concatenate([updated[:, 1:], arriving[:, None]], axis=1)
    return (block_out, noise_pred, new_queue)


def solution(mesh):
    placed = (
        P("seq", "queue", None),
        P("seq", "queue", None),
        P("seq", None),
        P("queue"),
        P(),
        P(),
        P(None, None, "seq"),
        P(None, "seq"),
        P(),
    )
    return jax.shard_map(
        shards,
        mesh=mesh,
        in_specs=placed,
        out_specs=(P("seq", "queue", None), P("seq", "queue", None), P("seq", "queue", None)),
        check_vma=False,
    )
```

profile of v0, /device:TPU:1, one launch (start us, length us, event | category | flops | bytes accessed | tf_op | source)
XLA Modules:
  0.0 224.5 jit_solution(14987704664879521586)
XLA Ops:
  9.2 23.0 %all_gather.6 = f32[3,2,3072]{2,1,0:T(2,128)S(1)} all-gather(f32[3,2,384]{2,1,0:T(2,128)S(1)} %convolution_bitcast_fusion.1), channel_id=1, replica_groups=mesh['queue'=32,'seq'=8] {'seq'}, dimensions={2}, use_global_device_ids=true | all-gather | bytes 82944 | tf_op jit(solution)/shard_map/all_gather | solution.py:115
  33.9 1.2 fusion.20
  35.2 2.0 fusion.23
  37.2 12.7 %copy.128 = bf16[3072,1536]{0,1:T(8,128)(2,1)} copy(bf16[3072,1536]{1,0:T(8,128)(2,1)} %param.18) | data formatting | bytes 18874368 | tf_op args[7]
  49.9 6.4 %slice.94 = bf16[3072,3,3,128]{0,3,2,1:T(8,128)(2,1)} slice(bf16[3072,3,4,128]{0,3,2,1:T(8,128)(2,1)} %bitcast.167), slice={[0:3072], [0:3], [0:3], [0:128]} | slice | bytes 14155776 | tf_op jit(solution)/shard_map/slice | solution.py:123
  56.3 3.3 %slice.98 = bf16[3072,3,1,128]{0,3,2,1:T(8,128)(2,1)} slice(bf16[3072,3,4,128]{0,3,2,1:T(8,128)(2,1)} %bitcast.168), slice={[0:3072], [0:3], [3:4], [0:128]} | slice | bytes 4718592 | tf_op jit(solution)/shard_map/slice | solution.py:124
  59.7 27.8 %all-gather.2.cloned.1.call-done = bf16[256,2,3072]{2,0,1:T(8,128)(2,1)} async-done(((bf16[32,2,3072]{2,0,1:T(8,128)(2,1)}), bf16[256,2,3072]{2,0,1:T(8,128)(2,1)}) %all-gather.2.cloned.1.call-update) | async-done | bytes 3145744 | tf_op jit(solution)/shard_map/all_gather | solution.py:127
  87.5 8.2 %convolution_convert_fusion.1 = bf16[256,2,1152]{2,0,1:T(8,128)(2,1)S(1)} fusion(bf16[256,2,3072]{2,0,1:T(8,128)(2,1)} %all-gather.2.cloned.1.call-done, bf16[3072,1152,1]{0,1,2:T(8,128)(2,1)} %bitcast.179), kind=kOutput, calls=%fused_computation.22 | convolution fusion | flops 3624468480 | bytes 11403264 | tf_op jit(solution)/shard_map/tfd,de->tfe/dot_general | solution.py:125
  98.5 7.8 %all-to-all-start = ((bf16[256,2,3,128]{3,1,2,0:T(2,128)(2,1)}), bf16[256,2,3,128]{3,1,2,0:T(2,128)(2,1)S(1)}, u32[]{:S(2)}, u32[]{:S(2)}) async-start(bf16[256,2,3,128]{3,1,2,0:T(2,128)(2,1)} %copy.134), calls=%async_computation | async-start | bytes 786432 | tf_op jit(solution)/shard_map/all_to_all | solution.py:154
  108.5 8.1 %all-to-all-done = bf16[256,2,3,128]{3,1,2,0:T(2,128)(2,1)S(1)} async-done(((bf16[256,2,3,128]{3,1,2,0:T(2,128)(2,1)}), bf16[256,2,3,128]{3,1,2,0:T(2,128)(2,1)S(1)}, u32[]{:S(2)}, u32[]{:S(2)}) %all-to-all-start) | async-done | bytes 393248 | tf_op jit(solution)/shard_map/all_to_all | solution.py:154
  116.6 3.7 %all-to-all-start.1 = ((bf16[256,2,3,128]{3,1,2,0:T(2,128)(2,1)}), bf16[256,2,3,128]{3,1,2,0:T(2,128)(2,1)S(1)}, u32[]{:S(2)}, u32[]{:S(2)}) async-start(bf16[256,2,3,128]{3,1,2,0:T(2,128)(2,1)} %copy.138), calls=%async_computation.1 | async-start | bytes 786432 | tf_op jit(solution)/shard_map/all_to_all | solution.py:153
  124.3 6.1 %all-to-all-done.1 = bf16[256,2,3,128]{3,1,2,0:T(2,128)(2,1)S(1)} async-done(((bf16[256,2,3,128]{3,1,2,0:T(2,128)(2,1)}), bf16[256,2,3,128]{3,1,2,0:T(2,128)(2,1)S(1)}, u32[]{:S(2)}, u32[]{:S(2)}) %all-to-all-start.1) | async-done | bytes 393248 | tf_op jit(solution)/shard_map/all_to_all | solution.py:153
  130.4 3.8 %all-to-all-start.2 = ((bf16[256,2,3,128]{3,1,2,0:T(2,128)(2,1)}), bf16[256,2,3,128]{3,1,2,0:T(2,128)(2,1)S(1)}, u32[]{:S(2)}, u32[]{:S(2)}) async-start(bf16[256,2,3,128]{3,1,2,0:T(2,128)(2,1)} %copy.142), calls=%async_computation.2 | async-start | bytes 786432 | tf_op jit(solution)/shard_map/all_to_all | solution.py:155
  134.4 4.5 %fusion.16 = f32[8,64,3,1,5]{4,3,2,1,0:T(1,128)S(1)} fusion(bf16[8,64,5,3,128]{4,0,3,1,2:T(8,128)(2,1)} %bitcast_dynamic-update-slice_fusion.4, bf16[8,64,3,128,1]{3,0,2,1,4:T(8,128)(2,1)S(1)} %bitcast.187), kind=kOutput, calls=%fused_computation.20 | convolution fusion | flops 1966080 | bytes 2390016 | tf_op jit(solution)/shard_map/rihe,ridhe->ridh/dot_general | solution.py:71
  141.2 3.1 %all-to-all-done.2 = bf16[256,2,3,128]{3,1,2,0:T(2,128)(2,1)S(1)} async-done(((bf16[256,2,3,128]{3,1,2,0:T(2,128)(2,1)}), bf16[256,2,3,128]{3,1,2,0:T(2,128)(2,1)S(1)}, u32[]{:S(2)}, u32[]{:S(2)}) %all-to-all-start.2) | async-done | bytes 393248 | tf_op jit(solution)/shard_map/all_to_all | solution.py:155
  144.8 2.9 %fusion.14 = f32[8,64,3,1,128]{4,3,2,1,0:T(1,128)S(1)} fusion(bf16[8,64,5,3,1]{2,4,3,1,0:T(2,128)(2,1)S(1)} %copy.159, bf16[8,64,5,3,128]{4,0,3,1,2:T(8,128)(2,1)S(1)} %bitcast_dynamic-update-slice_fusion), kind=kOutput, calls=%fused_computation.18 | convolution fusion | flops 1966080 | bytes 2767872 | tf_op jit(solution)/shard_map/ridh,ridhe->rihe/dot_general | solution.py:90
  147.7 1.3 fusion.26
  149.0 4.0 %all-to-all-start.3 = ((bf16[8,64,3,128]{3,0,2,1:T(8,128)(2,1)}), bf16[8,64,3,128]{3,0,2,1:T(8,128)(2,1)S(1)}, u32[]{:S(2)}, u32[]{:S(2)}) async-start(bf16[8,64,3,128]{3,0,2,1:T(8,128)(2,1)} %fusion.26), calls=%async_computation.3 | async-start | bytes 786432 | tf_op jit(solution)/shard_map/all_to_all | solution.py:160
  153.3 3.4 %while.10 = (s32[]{:T(128)}, f32[2,256,3,128]{3,1,2,0:T(8,128)}, bf16[2,256,3,128]{1,3,2,0:T(8,128)(2,1)S(1)}, bf16[2,256,3,128]{1,3,2,0:T(8,128)(2,1)S(1)}, bf16[2,256,3,128]{1,3,2,0:T(8,128)(2,1)S(1)}, /*index=5*/s32[]{:T(128)}) while((s32[]{:T(128)}, f32[2,256,3,128]{3,1,2,0:T(8,128)}, bf16[2,256,3,128]{1,3,2,0:T(8,128)(2,1)S(1)}, ...), condition=%wide.region_5.6_spmd, body=%wide.region_2.5_spmd.sunk | while | flops 101939712 | bytes 4934217 | solution.py:148
  156.7 6.6 %all-to-all-done.3 = bf16[8,64,3,128]{3,0,2,1:T(8,128)(2,1)S(1)} async-done(((bf16[8,64,3,128]{3,0,2,1:T(8,128)(2,1)}), bf16[8,64,3,128]{3,0,2,1:T(8,128)(2,1)S(1)}, u32[]{:S(2)}, u32[]{:S(2)}) %all-to-all-start.3) | async-done | bytes 393248 | tf_op jit(solution)/shard_map/all_to_all | solution.py:160
  164.9 3.4 %convolution_convert_fusion = bf16[512,3072]{1,0:T(8,128)(2,1)} fusion(bf16[3072,384]{0,1:T(8,128)(2,1)S(1)} %bitcast.181, bf16[64,8,3,128]{3,2,1,0:T(4,128)(2,1)S(1)} %bitcast.186), kind=kOutput, calls=%fused_computation.17 | convolution fusion | flops 1209532416 | bytes 5898240 | tf_op jit(solution)/shard_map/dot_general | solution.py:168
  169.0 38.2 %reduce-scatter.2.cloned.1.call-done = bf16[64,3072]{1,0:T(8,128)(2,1)} async-done(((bf16[512,3072]{1,0:T(8,128)(2,1)}), bf16[64,3072]{1,0:T(8,128)(2,1)}) %reduce-scatter.2.cloned.1.call-update) | async-done | bytes 393232 | tf_op jit(solution)/shard_map/reduce_scatter | solution.py:167
  207.2 1.5 reshape.213
  209.3 5.4 %collective-permute-start = (bf16[32,64]{1,0:T(8,128)(2,1)S(1)}, bf16[32,64]{1,0:T(8,128)(2,1)S(1)}, u32[]{:S(2)}, u32[]{:S(2)}) collective-permute-start(bf16[32,64]{1,0:T(8,128)(2,1)S(1)} %get-tuple-element.113), channel_id=1, source_target_pairs={{8,0},{16,8},{24,16},{32,24},{40,32},{48,40},{56,48},{64,56},{72,6... | collective-permute-start | bytes 12296 | tf_op jit(solution)/shard_map/ppermute | solution.py:21
  (86 shorter events, 25.0 us)
Async XLA Ops:
  7.2 201.8 %copy-start = (bf16[3072,64]{0,1:T(8,128)(2,1)S(1)}, bf16[3072,64]{0,1:T(8,128)(2,1)}, u32[]{:S(2)}) copy-start(bf16[3072,64]{0,1:T(8,128)(2,1)} %param.19) | copy-start | bytes 1179652
  7.2 80.3 %all-gather.2.cloned.1.call-start = ((), (), s32[]{:S(2)}) async-start(), calls=%async_computation.5 | async-start | bytes 3538944 | tf_op jit(solution)/shard_map/all_gather | solution.py:127
  56.3 3.3 %copy-start.7 = (s32[64]{0:T(128)S(1)}, s32[64]{0:T(128)}, u32[]{:S(2)}) copy-start(s32[64]{0:T(128)} %param.15) | copy-start | bytes 772
  96.4 9.9 %copy-start.8 = (s32[64]{0:T(128)S(1)}, s32[64]{0:T(128)}, u32[]{:S(2)}) copy-start(s32[64]{0:T(128)} %param.16) | copy-start | bytes 772
  98.5 18.1 %all-to-all-start = ((bf16[256,2,3,128]{3,1,2,0:T(2,128)(2,1)}), bf16[256,2,3,128]{3,1,2,0:T(2,128)(2,1)S(1)}, u32[]{:S(2)}, u32[]{:S(2)}) async-start(bf16[256,2,3,128]{3,1,2,0:T(2,128)(2,1)} %copy.134), calls=%async_computation | async-start | bytes 786432 | tf_op jit(solution)/shard_map/all_to_all | solution.py:154
  116.6 13.9 %all-to-all-start.1 = ((bf16[256,2,3,128]{3,1,2,0:T(2,128)(2,1)}), bf16[256,2,3,128]{3,1,2,0:T(2,128)(2,1)S(1)}, u32[]{:S(2)}, u32[]{:S(2)}) async-start(bf16[256,2,3,128]{3,1,2,0:T(2,128)(2,1)} %copy.138), calls=%async_computation.1 | async-start | bytes 786432 | tf_op jit(solution)/shard_map/all_to_all | solution.py:153
  130.4 13.9 %all-to-all-start.2 = ((bf16[256,2,3,128]{3,1,2,0:T(2,128)(2,1)}), bf16[256,2,3,128]{3,1,2,0:T(2,128)(2,1)S(1)}, u32[]{:S(2)}, u32[]{:S(2)}) async-start(bf16[256,2,3,128]{3,1,2,0:T(2,128)(2,1)} %copy.142), calls=%async_computation.2 | async-start | bytes 786432 | tf_op jit(solution)/shard_map/all_to_all | solution.py:155
  147.7 5.6 %copy-start.3 = (bf16[2,256,3,128]{1,3,2,0:T(8,128)(2,1)S(1)}, bf16[2,256,3,128]{1,3,2,0:T(8,128)(2,1)}, u32[]{:S(2)}) copy-start(bf16[2,256,3,128]{1,3,2,0:T(8,128)(2,1)} %get-tuple-element.162) | copy-start | bytes 1179652
  149.0 14.3 %all-to-all-start.3 = ((bf16[8,64,3,128]{3,0,2,1:T(8,128)(2,1)}), bf16[8,64,3,128]{3,0,2,1:T(8,128)(2,1)S(1)}, u32[]{:S(2)}, u32[]{:S(2)}) async-start(bf16[8,64,3,128]{3,0,2,1:T(8,128)(2,1)} %fusion.26), calls=%async_computation.3 | async-start | bytes 786432 | tf_op jit(solution)/shard_map/all_to_all | solution.py:160
  153.0 54.2 %reduce-scatter.2.cloned.1.call-start = ((), (), s32[]{:S(2)}) async-start(), calls=%async_computation.6 | async-start | bytes 3538944 | tf_op jit(solution)/shard_map/reduce_scatter | solution.py:167
  156.7 8.2 %copy-start.2 = (bf16[3072,3,1,128]{0,3,2,1:T(8,128)(2,1)S(1)}, bf16[3072,3,1,128]{0,3,2,1:T(8,128)(2,1)}, u32[]{:S(2)}) copy-start(bf16[3072,3,1,128]{0,3,2,1:T(8,128)(2,1)} %slice.98) | copy-start | bytes 7077892
  168.3 0.7 copy-start.9
  168.3 40.4 %copy-start.1 = (bf16[32,2,3072]{2,1,0:T(2,128)(2,1)S(1)}, bf16[32,2,3072]{2,1,0:T(2,128)(2,1)}, u32[]{:S(2)}) copy-start(bf16[32,2,3072]{2,1,0:T(2,128)(2,1)} %param.11) | copy-start | bytes 1179652
  168.3 40.4 %copy-start.4 = (f32[2,3072]{1,0:T(2,128)S(1)}, f32[2,3072]{1,0:T(2,128)}, u32[]{:S(2)}) copy-start(f32[2,3072]{1,0:T(2,128)} %get-tuple-element.107) | copy-start | bytes 73732
  169.0 40.0 %copy-start.5 = (bf16[32,2,64]{2,1,0:T(2,128)(2,1)S(1)}, bf16[32,2,64]{2,1,0:T(2,128)(2,1)}, u32[]{:S(2)}) copy-start(bf16[32,2,64]{2,1,0:T(2,128)(2,1)} %param.12) | copy-start | bytes 24580
  169.0 48.0 %copy-start.6 = (bf16[32,64]{1,0:T(8,128)(2,1)S(1)}, bf16[32,64]{1,0:T(8,128)(2,1)}, u32[]{:S(2)}) copy-start(bf16[32,64]{1,0:T(8,128)(2,1)} %param.13) | copy-start | bytes 12292
  209.3 7.7 %collective-permute-start = (bf16[32,64]{1,0:T(8,128)(2,1)S(1)}, bf16[32,64]{1,0:T(8,128)(2,1)S(1)}, u32[]{:S(2)}, u32[]{:S(2)}) collective-permute-start(bf16[32,64]{1,0:T(8,128)(2,1)S(1)} %get-tuple-element.113), channel_id=1, source_target_pairs={{8,0},{16,8},{24,16},{32,24},{40,32},{48,40},{56,48},{64,56},{72,6... | collective-permute-start | bytes 12296 | tf_op jit(solution)/shard_map/ppermute | solution.py:21
Sparse Core Ops, SparseCore 0:
  37.3 50.1 all-gather.1
  168.5 38.6 reduce-scatter.1
where the time goes:
time: 226 us; the launch traced here: 225 us
  waiting for transfers between devices  90.5 us (40%)
  local copies, waits for them, and re-layouts  40.9 us (18%)
  starting transfers between devices  25 us (11%)
  blocking collectives  23 us (10%)
  matrix products  21.7 us (10%)
  between operations  14.4 us (6%)
  other arithmetic  8.96 us (4%)
    reduce_scatter x1, waiting for transfers between devices, shards(): lax.psum_scatter(lax.dot_general(head_rows, out_weight, (((1,), (1,)), ((...  38.2 us
    all_gather x1, waiting for transfers between devices, shards(): lax.all_gather(normal, 'seq', axis=0, tiled=True)  27.8 us
    all_gather x1, blocking collectives, shards(): modulation = lax.all_gather(mod_part, 'seq', axis=2, tiled=True)  23 us
    unnamed x32, local copies, waits for them, and re-layouts  19.2 us
    dot_general x1, matrix products, shards(): jnp.einsum('tfd,de->tfe', lax.all_gather(normal, 'seq', axis=0, tiled=Tru...  8.22 us
    all_to_all x1, waiting for transfers between devices, shards(): lax.all_to_all(key_rows, 'queue', split_axis=0, concat_axis=1, tiled=True)  8.08 us
    all_to_all x1, starting transfers between devices, shards(): lax.all_to_all(key_rows, 'queue', split_axis=0, concat_axis=1, tiled=True)  7.77 us
    all_to_all x1, waiting for transfers between devices, shards(): lax.all_to_all(result.astype(jnp.bfloat16), 'queue', split_axis=1, concat...  6.65 us
  transfers between devices with their start and end apart: 7, of which 7 were waited for; matrix products, arithmetic and copies ran while one was open for 18% of the time, Pallas kernels for 0%

commit v1 on v0

v1 whole, which is shorter than its diff:
```python
import functools
import math

import jax
import jax.numpy as jnp
from jax import lax
from jax.experimental import pallas as pl
from jax.experimental.pallas import tpu as pltpu
from jax.sharding import PartitionSpec as P

HD = 128
STRIDE = 16
WMAX = 2

LN_EPS = 1e-06
DECAY = 2.3
NEAR_COST = 0.5

MESH = pl.DeviceIdType.MESH
F32 = jnp.float32
BF16 = jnp.bfloat16
NT = (((1,), (1,)), ((), ()))


def kernel(
    Q,
    Z,
    hid,
    lat,
    fresh,
    steps,
    slots,
    wins,
    mw_hbm,
    w_hbm,
    fw_hbm,
    out,
    pred,
    queue,
    xs,
    wqkv,
    wout,
    mw,
    fw,
    part,
    mod,
    norm,
    qb,
    kv,
    hd,
    sent_r,
    sent_l,
    in_r,
    in_l,
    upd,
    got,
    w_sem,
    mw_sem,
    fw_sem,
    mod_send,
    mod_recv,
    ag_send,
    ag_recv,
    halo_send,
    halo_recv,
    rs_send,
    rs_recv,
    edge_send,
    edge_recv,
):
    F, T, D = hid.shape
    LH = w_hbm.shape[1] // (4 * HD)
    MP = mw_hbm.shape[2]
    FREQ = mw_hbm.shape[1]
    FRAMES = F * Q
    factor = 1.0 / math.sqrt(HD)
    z = lax.axis_index("seq")
    q = lax.axis_index("queue")
    z_right, z_left = lax.rem(z + 1, Z), lax.rem(z + Z - 1, Z)
    q_right, q_left = lax.rem(q + 1, Q), lax.rem(q + Q - 1, Q)

    def weight_copies():
        copies = []
        for h in range(LH):
            copies.append(
                pltpu.make_async_copy(
                    w_hbm.at[:, pl.ds(h * 4 * HD, 3 * HD)],
                    wqkv.at[:, pl.ds(h * 3 * HD, 3 * HD)],
                    w_sem.at[h],
                )
            )
        for h in range(LH):
            copies.append(
                pltpu.make_async_copy(
                    w_hbm.at[:, pl.ds(h * 4 * HD + 3 * HD, HD)],
                    wout.at[:, pl.ds(h * HD, HD)],
                    w_sem.at[LH + h],
                )
            )
        return copies

    weights = weight_copies()
    mw_copy = pltpu.make_async_copy(mw_hbm, mw, mw_sem)
    fw_copy = pltpu.make_async_copy(fw_hbm, fw, fw_sem)
    mw_copy.start()
    for copy in weights:
        copy.start()
    fw_copy.start()

    barrier = pltpu.get_barrier_semaphore()
    for k in range(1, Z):
        pl.semaphore_signal(
            barrier, inc=1, device_id=(q, lax.rem(z + k, Z)), device_id_type=MESH
        )
    for other in (q_left, q_right):
        pl.semaphore_signal(barrier, inc=1, device_id=(other, z), device_id_type=MESH)
    pl.semaphore_wait(barrier, Z + 1)

    def gather_copy(way, u, src, chunk, frame):
        return pltpu.make_async_remote_copy(
            src_ref=src,
            dst_ref=xs.at[chunk, frame],
            send_sem=ag_send.at[way, u],
            recv_sem=ag_recv.at[way, u],
            device_id=(q, z_right if way == 0 else z_left),
            device_id_type=MESH,
        )

    for u in (1, 2):
        gather_copy(0, u, hid.at[u - 1], z, u - 1).start()
        gather_copy(1, u, hid.at[2 - u], z, 2 - u).start()

    xs[z] = hid[...]
    for slot in (0, 1):
        in_r[slot] = jnp.zeros((T, D), BF16)
        in_l[slot] = jnp.zeros((T, D), BF16)

    rows = lax.broadcasted_iota(jnp.int32, (8, FREQ), 0)
    lanes = lax.broadcasted_iota(jnp.int32, (8, FREQ), 1)
    half = FREQ // 2
    ladder = jnp.exp(lax.rem(lanes, half).astype(F32) * (-math.log(10000.0) / half))
    ids = jnp.where(lax.rem(rows, 2) == 0, steps[0], steps[1])
    angles = ids.astype(F32) * ladder
    freq = jnp.where(lanes < half, jnp.cos(angles), jnp.sin(angles))
    temb = (freq / (1.0 + jnp.exp(-freq))).astype(BF16)
    mw_copy.wait()
    rows = lax.broadcasted_iota(jnp.int32, (8, MP), 0)
    maps = [jnp.dot(temb, mw[p], preferred_element_type=F32) for p in range(3)]
    part[...] = jnp.where(rows < 2, maps[0], jnp.where(rows < 4, maps[1], maps[2]))

    def mod_copy(k, owner):
        return pltpu.make_async_remote_copy(
            src_ref=part,
            dst_ref=mod.at[:, pl.ds(pl.multiple_of(owner * MP, MP), MP)],
            send_sem=mod_send.at[k],
            recv_sem=mod_recv.at[k],
            device_id=(q, lax.rem(z + k, Z)),
            device_id_type=MESH,
        )

    for k in range(1, Z):
        mod_copy(k, z).start()
    mod[:, pl.ds(pl.multiple_of(z * MP, MP), MP)] = part[...]
    for k in range(1, Z):
        mod_copy(k, lax.rem(z + Z - k, Z)).wait_recv()
    for copy in weights:
        copy.wait()

    def normalise(chunk, frame, base):
        scale = 1.0 + mod[pl.ds(2 + frame, 1), :]
        shift = mod[pl.ds(frame, 1), :]
        for r in range(0, T, 16):
            x = xs[chunk, frame, r : r + 16, :].astype(F32)
            centred = x - jnp.sum(x, axis=1, keepdims=True) * (1.0 / D)
            variance = jnp.sum(centred * centred, axis=1, keepdims=True) * (1.0 / D)
            y = centred * lax.rsqrt(variance + LN_EPS) * scale + shift
            norm[base + r : base + r + 16, :] = y.astype(BF16)

    def halo_copy(side, u, i, chunk, frame):
        rows_here = pl.ds(pl.multiple_of(chunk * T, T), T)
        return pltpu.make_async_remote_copy(
            src_ref=kv.at[F + frame, rows_here],
            dst_ref=kv.at[frame + (0 if side == 0 else 2 * F), rows_here],
            send_sem=halo_send.at[side, i, u],
            recv_sem=halo_recv.at[side, i, u],
            device_id=(q_right if side == 0 else q_left, z),
            device_id_type=MESH,
        )

    def gather_place(u):
        step = (u + 1) // 2
        left = (lax.rem(z + Z - step, Z), lax.rem(u + 1, 2))
        right = (lax.rem(z + step, Z), lax.rem(u, 2))
        return left, right

    def gather_unit(u, carry):
        places = gather_place(u)

        @pl.when(u >= 1)
        def _():
            for way in (0, 1):
                chunk, frame = places[way]
                gather_copy(way, u, xs.at[chunk, frame], chunk, frame).wait_recv()

                @pl.when(u + 2 <= Z - 1)
                def _():
                    gather_copy(way, u + 2, xs.at[chunk, frame], chunk, frame).start()

        for way in (0, 1):
            normalise(*places[way], way * T)
        projected = jnp.dot(norm[...], wqkv[...], preferred_element_type=F32).astype(BF16)
        for way in (0, 1):
            chunk, frame = places[way]
            rows_here = pl.ds(pl.multiple_of(chunk * T, T), T)
            block = projected[way * T : (way + 1) * T]
            for h in range(LH):
                at = h * 3 * HD
                qb[frame, rows_here, h * HD : (h + 1) * HD] = block[:, at : at + HD]
                kv[F + frame, rows_here, h * 2 * HD : (h + 1) * 2 * HD] = block[
                    :, at + HD : at + 3 * HD
                ]
            for side in (0, 1):
                halo_copy(side, u, way, chunk, frame).start()
        return carry

    lax.fori_loop(0, Z, gather_unit, 0)

    def halo_wait(u, carry):
        places = gather_place(u)
        for way in (0, 1):
            for side in (0, 1):
                halo_copy(side, u, way, *places[way]).wait_recv()
        return carry

    def spatial(chunk, frame):
        rows_here = pl.ds(pl.multiple_of(chunk * T, T), T)
        results = []
        for h in range(LH):
            queries = qb[frame, rows_here, h * HD : (h + 1) * HD]
            keys = kv[F + frame, :, h * 2 * HD : h * 2 * HD + HD]
            values = kv[F + frame, :, h * 2 * HD + HD : (h + 1) * 2 * HD]
            scores = lax.dot_general(queries, keys, NT, preferred_element_type=F32) * factor
            expo = jnp.exp(scores - jnp.max(scores, axis=1, keepdims=True))
            total = jnp.sum(expo, axis=1, keepdims=True)
            mixed = jnp.dot(expo.astype(BF16), values, preferred_element_type=F32)
            results.append(mixed / total)
        return results

    def temporal(chunk, frame):
        rows_here = pl.ds(pl.multiple_of(chunk * T, T), T)
        here = q * F + frame
        slot = slots[here]
        window = wins[here]
        gates = []
        for d in range(-WMAX, WMAX + 1):
            there = here + d
            inside = jnp.logical_and(there >= 0, there < FRAMES)
            gap = jnp.abs(slots[jnp.clip(there, 0, FRAMES - 1)] - slot)
            gates.append((jnp.logical_and(inside, gap <= window), gap.astype(F32) * NEAR_COST))
        results = []
        for h in range(LH):
            queries = qb[frame, rows_here, h * HD : (h + 1) * HD].astype(F32)
            logits = []
            for d in range(2 * WMAX + 1):
                keys = kv[F + frame + d - WMAX, rows_here, h * 2 * HD : h * 2 * HD + HD]
                score = jnp.sum(queries * keys.astype(F32), axis=1, keepdims=True) * factor
                allowed, cost = gates[d]
                logits.append(jnp.where(allowed, score - cost, -1e30))
            peak = functools.reduce(jnp.maximum, logits)
            total = jnp.zeros((T, 1), F32)
            mixed = jnp.zeros((T, HD), F32)
            for d in range(2 * WMAX + 1):
                weight = jnp.where(gates[d][0], jnp.exp(logits[d] - peak), 0.0)
                values = kv[
                    F + frame + d - WMAX, rows_here, h * 2 * HD + HD : (h + 1) * 2 * HD
                ]
                total = total + weight
                mixed = mixed + weight * values.astype(F32)
            results.append(mixed / total)
        return results

    def scatter_copy(way, n):
        src, dst = (sent_r, in_r) if way == 0 else (sent_l, in_l)
        return pltpu.make_async_remote_copy(
            src_ref=src.at[n - 1],
            dst_ref=dst.at[n + 1],
            send_sem=rs_send.at[way, n],
            recv_sem=rs_recv.at[way, n],
            device_id=(q, z_right if way == 0 else z_left),
            device_id_type=MESH,
        )

    def scatter_unit(n, carry):
        step = Z // 2 - n // 2
        right = (lax.rem(z + step, Z), lax.rem(n + 1, 2))
        left = (lax.rem(z + Z - step, Z), lax.rem(n, 2))
        spread = [spatial(*right), spatial(*left)]

        @pl.when(n == 1)
        def _():
            lax.fori_loop(0, Z, halo_wait, 0)

        along = [temporal(*right), temporal(*left)]
        for i in (0, 1):
            for h in range(LH):
                hd[i * T : (i + 1) * T, h * HD : (h + 1) * HD] = (
                    spread[i][h] + along[i][h]
                ).astype(BF16)

        @pl.when(n >= 3)
        def _():
            for way in (0, 1):
                scatter_copy(way, n - 2).wait_recv()

        tile = 512
        for c in range(0, D, tile):
            share = lax.dot_general(hd[...], wout[c : c + tile, :], NT, preferred_element_type=F32)
            sent_r[n - 1, :, c : c + tile] = (
                share[:T] + in_r[n - 1, :, c : c + tile].astype(F32)
            ).astype(BF16)
            sent_l[n - 1, :, c : c + tile] = (
                share[T:] + in_l[n - 1, :, c : c + tile].astype(F32)
            ).astype(BF16)

        @pl.when(n <= Z - 1)
        def _():
            for way in (0, 1):
                scatter_copy(way, n).start()

        return carry

    lax.fori_loop(1, Z + 1, scatter_unit, 0)

    fw_copy.wait()
    horizon = STRIDE * (FRAMES + 1)
    LAT = lat.shape[2]

    def schedule(f):
        ids = jnp.full((T, LAT), steps[f], jnp.int32)
        now = jnp.exp(ids.astype(F32) * (-DECAY / horizon))
        before = jnp.exp((ids - STRIDE).astype(F32) * (-DECAY / horizon))
        return jnp.sqrt(1.0 - now), jnp.sqrt(now), jnp.sqrt(before), jnp.sqrt(1.0 - before)

    tables = [schedule(f) for f in range(F)]
    for way in (0, 1):
        scatter_copy(way, Z - 1).wait_recv()
    edge = pltpu.make_async_remote_copy(
        src_ref=upd,
        dst_ref=got,
        send_sem=edge_send,
        recv_sem=edge_recv,
        device_id=(q_left, z),
        device_id_type=MESH,
    )
    for f, (mine, theirs) in enumerate(((sent_l, in_r), (sent_r, in_l))):
        total = mine[Z - 1].astype(F32) + theirs[Z].astype(F32)
        gate = mod[4 + f : 5 + f, :]
        block = (hid[f].astype(F32) + gate * total).astype(BF16)
        out[f] = block
        noise = lax.dot_general(block, fw[...], NT, preferred_element_type=F32)
        pred[f] = noise.astype(BF16)
        noise_now, root_now, root_before, noise_before = tables[f]
        clean = (lat[f].astype(F32) - noise_now * noise) / root_now
        updated = (root_before * clean + noise_before * noise).astype(BF16)
        if f == 0:
            upd[...] = updated
            edge.start()
        else:
            queue[f - 1] = updated
    edge.wait_recv()
    queue[F - 1] = jnp.where(q == Q - 1, fresh[...], got[...])

    edge.wait_send()
    for k in range(1, Z):
        mod_copy(k, z).wait_send()

    def drain(u, carry):
        places = gather_place(u)
        for way in (0, 1):
            chunk, frame = places[way]

            @pl.when(u >= 1)
            def _():
                gather_copy(way, u, xs.at[chunk, frame], chunk, frame).wait_send()
                scatter_copy(way, u).wait_send()

            for side in (0, 1):
                halo_copy(side, u, way, chunk, frame).wait_send()
        return carry

    lax.fori_loop(0, Z, drain, 0)


def shards(
    Q,
    Z,
    hidden,
    latent,
    fresh_noise,
    timesteps,
    queue_slots,
    windows,
    mod_weight,
    attention_weight,
    final_weight,
):
    T, F, D = hidden.shape
    LAT = latent.shape[2]
    W = attention_weight.shape[1]
    MP = mod_weight.shape[2]
    vmem = pl.BlockSpec(memory_space=pltpu.VMEM)
    smem = pl.BlockSpec(memory_space=pltpu.SMEM)
    hbm = pl.BlockSpec(memory_space=pl.ANY)
    dma = pltpu.SemaphoreType.DMA
    out, pred, queue = pl.pallas_call(
        functools.partial(kernel, Q, Z),
        out_shape=(
            jax.ShapeDtypeStruct((F, T, D), BF16),
            jax.ShapeDtypeStruct((F, T, LAT), BF16),
            jax.ShapeDtypeStruct((F, T, LAT), BF16),
        ),
        in_specs=[vmem, vmem, vmem, smem, smem, smem, hbm, hbm, hbm],
        out_specs=(vmem, vmem, vmem),
        scratch_shapes=[
            pltpu.VMEM((Z, F, T, D), BF16),
            pltpu.VMEM((D, W // 4 * 3), BF16),
            pltpu.VMEM((D, W // 4), BF16),
            pltpu.VMEM(mod_weight.shape, BF16),
            pltpu.VMEM((LAT, D), BF16),
            pltpu.VMEM((8, MP), F32),
            pltpu.VMEM((8, D), F32),
            pltpu.VMEM((2 * T, D), BF16),
            pltpu.VMEM((F, Z * T, W // 4), BF16),
            pltpu.VMEM((3 * F, Z * T, W // 2), BF16),
            pltpu.VMEM((2 * T, W // 4), BF16),
            pltpu.VMEM((Z, T, D), BF16),
            pltpu.VMEM((Z, T, D), BF16),
            pltpu.VMEM((Z + 1, T, D), BF16),
            pltpu.VMEM((Z + 1, T, D), BF16),
            pltpu.VMEM((T, LAT), BF16),
            pltpu.VMEM((T, LAT), BF16),
            dma((2 * (W // (4 * HD)),)),
            dma,
            dma,
            dma((Z,)),
            dma((Z,)),
            dma((2, Z)),
            dma((2, Z)),
            dma((2, 2, Z)),
            dma((2, 2, Z)),
            dma((2, Z)),
            dma((2, Z)),
            dma,
            dma,
        ],
        compiler_params=pltpu.CompilerParams(
            collective_id=0, has_side_effects=True, vmem_limit_bytes=56 * 1024 * 1024
        ),
        cost_estimate=pl.CostEstimate(
            flops=2 * Z * T * F * D * W, bytes_accessed=2 * D * W, transcendentals=0
        ),
    )(
        jnp.swapaxes(hidden, 0, 1),
        jnp.swapaxes(latent, 0, 1),
        fresh_noise,
        timesteps,
        queue_slots,
        windows,
        mod_weight,
        attention_weight,
        jnp.transpose(final_weight),
    )
    return jnp.swapaxes(out, 0, 1), jnp.swapaxes(pred, 0, 1), jnp.swapaxes(queue, 0, 1)


def solution(mesh):
    placed = (
        P("seq", "queue", None),
        P("seq", "queue", None),
        P("seq", None),
        P("queue"),
        P(),
        P(),
        P(None, None, "seq"),
        P(None, "seq"),
        P(),
    )
    return jax.shard_map(
        functools.partial(shards, mesh.shape["queue"], mesh.shape["seq"]),
        mesh=mesh,
        in_specs=placed,
        out_specs=(P("seq", "queue", None), P("seq", "queue", None), P("seq", "queue", None)),
        check_vma=False,
    )
```

time: 226 us -> 96.9 us (0.43)
  waiting for transfers between devices: 90.5 us -> 0 us
  Pallas kernels: 0 us -> 87.5 us
  local copies, waits for them, and re-layouts: 40.9 us -> 7.95 us
  starting transfers between devices: 25 us -> 0 us
  blocking collectives: 23 us -> 0 us
  matrix products: 21.7 us -> 0 us
  between operations: 14.4 us -> 0.64 us
  other arithmetic: 8.96 us -> 0 us
    pallas_call x0 -> x1, Pallas kernels: none -> 87.5 us  [shards(): pl.pallas_call(functools.partial(kernel, Q, Z), out_shape=(jax.ShapeDtype...]
    reduce_scatter x1 -> x0, waiting for transfers between devices: 38.2 us -> none  [shards(): lax.psum_scatter(lax.dot_general(head_rows, out_weight, (((1,), (1,)), ((...]
    all_gather x1 -> x0, waiting for transfers between devices: 27.8 us -> none  [shards(): lax.all_gather(normal, 'seq', axis=0, tiled=True)]
    all_to_all x4 -> x0, waiting for transfers between devices: 23.9 us -> none  [the longest x1 8.08 us: shards(): lax.all_to_all(key_rows, 'queue', split_axis=0, concat_axis=1, tiled=True)]
    all_gather x1 -> x0, blocking collectives: 23 us -> none  [shards(): modulation = lax.all_gather(mod_part, 'seq', axis=2, tiled=True)]
    dot_general x10 -> x0, matrix products: 21.7 us -> none  [the longest x1 8.22 us: shards(): jnp.einsum('tfd,de->tfe', lax.all_gather(normal, 'seq', axis=0, tiled=Tru...]
    all_to_all x4 -> x0, starting transfers between devices: 19.3 us -> none  [the longest x1 7.77 us: shards(): lax.all_to_all(key_rows, 'queue', split_axis=0, concat_axis=1, tiled=True)]
    unnamed x32 -> x5, local copies, waits for them, and re-layouts: 19.2 us -> 7.95 us
  transfers between devices with their start and end apart: 7 -> 0, of which waited for: 7 -> 0; matrix products, arithmetic and copies ran while one was open for 18% -> 0% of each run, Pallas kernels for 0% -> 0%
where the time goes in v1:
time: 96.9 us; the launch traced here: 96.1 us
  Pallas kernels  87.5 us (90%)
  local copies, waits for them, and re-layouts  7.95 us (8%)
    pallas_call x1, Pallas kernels, shards(): pl.pallas_call(functools.partial(kernel, Q, Z), out_shape=(jax.ShapeDtype...  87.5 us
    unnamed x5, local copies, waits for them, and re-layouts  7.95 us

profile of v1, /device:TPU:1, one launch (start us, length us, event | category | flops | bytes accessed | tf_op | source)
XLA Modules:
  0.0 96.1 jit_solution(7852366128244297949)
XLA Ops:
  0.6 1.3 %copy.20 = bf16[32,2,64]{2,0,1:T(8,128)(2,1)} copy(bf16[32,2,64]{2,1,0:T(2,128)(2,1)} %param.10) | data formatting | bytes 16384 | tf_op args[1]
  2.0 1.8 %copy.19 = bf16[32,2,3072]{2,0,1:T(8,128)(2,1)} copy(bf16[32,2,3072]{2,1,0:T(2,128)(2,1)} %param.9) | data formatting | bytes 786432 | tf_op args[0]
  3.8 87.5 %shard_map.112 = (bf16[2,32,3072]{2,1,0:T(8,128)(2,1)}, bf16[2,32,64]{2,1,0:T(8,128)(2,1)}, bf16[2,32,64]{2,1,0:T(8,128)(2,1)}) custom-call(bf16[2,32,3072]{2,1,0:T(8,128)(2,1)} %bitcast.11, bf16[2,32,64]{2,1,0:T(8,128)(2,1)} %bitcast.14, bf16[32,64]{1,0:T(8,128)(2,1)} %fresh.1, s32[2]{0:T(128)} %steps.1, s32[64]{0:T(128)} %slots.1, s32[64]{0:T(128)} %wins.1, ...), custom_call_target="tpu_custom_call" | custom-call | flops 4831838208 | bytes 9437184 | tf_op jit(solution)/shard_map/pallas_call | solution.py:415
  91.2 2.1 %copy.14 = bf16[32,2,3072]{2,1,0:T(2,128)(2,1)} copy(bf16[32,2,3072]{2,0,1:T(8,128)(2,1)} %bitcast.10) | data formatting | bytes 786432
  93.4 1.3 %copy.15 = bf16[32,2,64]{2,1,0:T(2,128)(2,1)} copy(bf16[32,2,64]{2,0,1:T(8,128)(2,1)} %bitcast.13) | data formatting | bytes 16384
  94.7 1.3 %copy.16 = bf16[32,2,64]{2,1,0:T(2,128)(2,1)} copy(bf16[32,2,64]{2,0,1:T(8,128)(2,1)} %bitcast.12) | data formatting | bytes 16384

commit v2 on v1

--- a/solution.py
+++ b/solution.py
@@ -25,7 +25,7 @@
 def kernel(
     Q,
     Z,
-    hid,
+    hid_hbm,
     lat,
     fresh,
     steps,
@@ -37,6 +37,7 @@
     out,
     pred,
     queue,
+    raw,
     xs,
     wqkv,
     wout,
@@ -48,12 +49,14 @@
     qb,
     kv,
     hd,
+    share,
     sent_r,
     sent_l,
     in_r,
     in_l,
     upd,
     got,
+    hid_sem,
     w_sem,
     mw_sem,
     fw_sem,
@@ -68,7 +71,7 @@
     edge_send,
     edge_recv,
 ):
-    F, T, D = hid.shape
+    T, F, D = hid_hbm.shape
     LH = w_hbm.shape[1] // (4 * HD)
     MP = mw_hbm.shape[2]
     FREQ = mw_hbm.shape[1]
@@ -99,14 +102,6 @@
             )
         return copies
 
-    weights = weight_copies()
-    mw_copy = pltpu.make_async_copy(mw_hbm, mw, mw_sem)
-    fw_copy = pltpu.make_async_copy(fw_hbm, fw, fw_sem)
-    mw_copy.start()
-    for copy in weights:
-        copy.start()
-    fw_copy.start()
-
     barrier = pltpu.get_barrier_semaphore()
     for k in range(1, Z):
         pl.semaphore_signal(
@@ -114,7 +109,16 @@
         )
     for other in (q_left, q_right):
         pl.semaphore_signal(barrier, inc=1, device_id=(other, z), device_id_type=MESH)
-    pl.semaphore_wait(barrier, Z + 1)
+
+    weights = weight_copies()
+    hid_copy = pltpu.make_async_copy(hid_hbm, raw, hid_sem)
+    mw_copy = pltpu.make_async_copy(mw_hbm, mw, mw_sem)
+    fw_copy = pltpu.make_async_copy(fw_hbm, fw, fw_sem)
+    hid_copy.start()
+    mw_copy.start()
+    for copy in weights:
+        copy.start()
+    fw_copy.start()
 
     def gather_copy(way, u, src, chunk, frame):
         return pltpu.make_async_remote_copy(
@@ -126,11 +130,6 @@
             device_id_type=MESH,
         )
 
-    for u in (1, 2):
-        gather_copy(0, u, hid.at[u - 1], z, u - 1).start()
-        gather_copy(1, u, hid.at[2 - u], z, 2 - u).start()
-
-    xs[z] = hid[...]
     for slot in (0, 1):
         in_r[slot] = jnp.zeros((T, D), BF16)
         in_l[slot] = jnp.zeros((T, D), BF16)
@@ -158,13 +157,21 @@
             device_id_type=MESH,
         )
 
+    hid_copy.wait()
+    rows = lax.broadcasted_iota(jnp.int32, (F * T, F * T), 0)
+    cols = lax.broadcasted_iota(jnp.int32, (F * T, F * T), 1)
+    pick = (cols == F * lax.rem(rows, T) + lax.div(rows, T)).astype(BF16)
+    by_frame = jnp.dot(pick, raw[...].reshape(F * T, D), preferred_element_type=F32).astype(BF16)
+    for f in range(F):
+        xs[z, f] = by_frame[f * T : (f + 1) * T]
+
+    pl.semaphore_wait(barrier, Z + 1)
     for k in range(1, Z):
         mod_copy(k, z).start()
+    for u in (1, 2):
+        gather_copy(0, u, xs.at[z, u - 1], z, u - 1).start()
+        gather_copy(1, u, xs.at[z, 2 - u], z, 2 - u).start()
     mod[:, pl.ds(pl.multiple_of(z * MP, MP), MP)] = part[...]
-    for k in range(1, Z):
-        mod_copy(k, lax.rem(z + Z - k, Z)).wait_recv()
-    for copy in weights:
-        copy.wait()
 
     def normalise(chunk, frame, base):
         scale = 1.0 + mod[pl.ds(2 + frame, 1), :]
@@ -193,18 +200,25 @@
         right = (lax.rem(z + step, Z), lax.rem(u, 2))
         return left, right
 
+    def pass_on(u):
+        places = gather_place(u)
+        for way in (0, 1):
+            chunk, frame = places[way]
+            gather_copy(way, u, xs.at[chunk, frame], chunk, frame).wait_recv()
+
+            @pl.when(u + 2 <= Z - 1)
+            def _():
+                gather_copy(way, u + 2, xs.at[chunk, frame], chunk, frame).start()
+
+    pass_on(1)
+    for k in range(1, Z):
+        mod_copy(k, lax.rem(z + Z - k, Z)).wait_recv()
+    for copy in weights:
+        copy.wait()
+
     def gather_unit(u, carry):
         places = gather_place(u)
-
-        @pl.when(u >= 1)
-        def _():
-            for way in (0, 1):
-                chunk, frame = places[way]
-                gather_copy(way, u, xs.at[chunk, frame], chunk, frame).wait_recv()
-
-                @pl.when(u + 2 <= Z - 1)
-                def _():
-                    gather_copy(way, u + 2, xs.at[chunk, frame], chunk, frame).start()
+        pl.when(u >= 2)(lambda: pass_on(u))
 
         for way in (0, 1):
             normalise(*places[way], way * T)
@@ -279,20 +293,24 @@
             results.append(mixed / total)
         return results
 
-    def scatter_copy(way, n):
+    half = T // 2
+
+    def scatter_copy(way, n, part_of):
         src, dst = (sent_r, in_r) if way == 0 else (sent_l, in_l)
+        rows_here = pl.ds(part_of * half, half)
         return pltpu.make_async_remote_copy(
-            src_ref=src.at[n - 1],
-            dst_ref=dst.at[n + 1],
-            send_sem=rs_send.at[way, n],
-            recv_sem=rs_recv.at[way, n],
+            src_ref=src.at[n - 1, rows_here],
+            dst_ref=dst.at[n + 1, rows_here],
+            send_sem=rs_send.at[way, part_of, n],
+            recv_sem=rs_recv.at[way, part_of, n],
             device_id=(q, z_right if way == 0 else z_left),
             device_id_type=MESH,
         )
 
     def scatter_unit(n, carry):
         step = Z // 2 - n // 2
-        right = (lax.rem(z + step, Z), lax.rem(n + 1, 2))
+        late = n // (Z - 2) - n // Z
+        right = (lax.rem(z + step, Z), lax.rem(n + 1 + late, 2))
         left = (lax.rem(z + Z - step, Z), lax.rem(n, 2))
         spread = [spatial(*right), spatial(*left)]
 
@@ -306,26 +324,29 @@
                 hd[i * T : (i + 1) * T, h * HD : (h + 1) * HD] = (
                     spread[i][h] + along[i][h]
                 ).astype(BF16)
-
-        @pl.when(n >= 3)
-        def _():
-            for way in (0, 1):
-                scatter_copy(way, n - 2).wait_recv()
-
         tile = 512
         for c in range(0, D, tile):
-            share = lax.dot_general(hd[...], wout[c : c + tile, :], NT, preferred_element_type=F32)
-            sent_r[n - 1, :, c : c + tile] = (
-                share[:T] + in_r[n - 1, :, c : c + tile].astype(F32)
-            ).astype(BF16)
-            sent_l[n - 1, :, c : c + tile] = (
-                share[T:] + in_l[n - 1, :, c : c + tile].astype(F32)
-            ).astype(BF16)
+            share[:, c : c + tile] = lax.dot_general(
+                hd[...], wout[c : c + tile, :], NT, preferred_element_type=F32
+            )
 
         @pl.when(n <= Z - 1)
         def _():
-            for way in (0, 1):
-                scatter_copy(way, n).start()
+            needs = (n - 2 + late * (2 * Z - 3 - 2 * n), n - 2)
+            for part_of in (0, 1):
+                for way, (sent, arrived) in enumerate(((sent_r, in_r), (sent_l, in_l))):
+                    need = needs[way]
+
+                    @pl.when(n >= 3)
+                    def _():
+                        scatter_copy(way, need, part_of).wait_recv()
+
+                    mine = way * T + part_of * half
+                    rows_here = slice(part_of * half, (part_of + 1) * half)
+                    sent[n - 1, rows_here, :] = (
+                        share[mine : mine + half, :] + arrived[need + 1, rows_here, :].astype(F32)
+                    ).astype(BF16)
+                    scatter_copy(way, n, part_of).start()
 
         return carry
 
@@ -342,8 +363,6 @@
         return jnp.sqrt(1.0 - now), jnp.sqrt(now), jnp.sqrt(before), jnp.sqrt(1.0 - before)
 
     tables = [schedule(f) for f in range(F)]
-    for way in (0, 1):
-        scatter_copy(way, Z - 1).wait_recv()
     edge = pltpu.make_async_remote_copy(
         src_ref=upd,
         dst_ref=got,
@@ -352,15 +371,23 @@
         device_id=(q_left, z),
         device_id_type=MESH,
     )
-    for f, (mine, theirs) in enumerate(((sent_l, in_r), (sent_r, in_l))):
-        total = mine[Z - 1].astype(F32) + theirs[Z].astype(F32)
+    for f in range(F):
+        for way in (0, 1):
+            for part_of in (0, 1):
+                scatter_copy(way, Z - 2 + f, part_of).wait_recv()
+        mine = (1 - f) * T
+        total = (
+            share[mine : mine + T, :]
+            + in_r[Z - 1 + f].astype(F32)
+            + in_l[Z - 1 + f].astype(F32)
+        )
         gate = mod[4 + f : 5 + f, :]
-        block = (hid[f].astype(F32) + gate * total).astype(BF16)
+        block = (xs[z, f].astype(F32) + gate * total).astype(BF16)
         out[f] = block
         noise = lax.dot_general(block, fw[...], NT, preferred_element_type=F32)
         pred[f] = noise.astype(BF16)
         noise_now, root_now, root_before, noise_before = tables[f]
-        clean = (lat[f].astype(F32) - noise_now * noise) / root_now
+        clean = (lat[:, f, :].astype(F32) - noise_now * noise) / root_now
         updated = (root_before * clean + noise_before * noise).astype(BF16)
         if f == 0:
             upd[...] = updated
@@ -382,13 +409,20 @@
             @pl.when(u >= 1)
             def _():
                 gather_copy(way, u, xs.at[chunk, frame], chunk, frame).wait_send()
-                scatter_copy(way, u).wait_send()
+                for part_of in (0, 1):
+                    scatter_copy(way, u, part_of).wait_send()
 
             for side in (0, 1):
                 halo_copy(side, u, way, chunk, frame).wait_send()
         return carry
 
     lax.fori_loop(0, Z, drain, 0)
+
+
+def by_token(*refs):
+    for src, dst in zip(refs[:3], refs[3:]):
+        for f in range(src.shape[0]):
+            dst[:, f, :] = src[f]
 
 
 def shards(
@@ -410,7 +444,7 @@
     MP = mod_weight.shape[2]
     vmem = pl.BlockSpec(memory_space=pltpu.VMEM)
     smem = pl.BlockSpec(memory_space=pltpu.SMEM)
-    hbm = pl.BlockSpec(memory_space=pl.ANY)
+    hbm = pl.BlockSpec(memory_space=pltpu.HBM)
     dma = pltpu.SemaphoreType.DMA
     out, pred, queue = pl.pallas_call(
         functools.partial(kernel, Q, Z),
@@ -419,9 +453,10 @@
             jax.ShapeDtypeStruct((F, T, LAT), BF16),
             jax.ShapeDtypeStruct((F, T, LAT), BF16),
         ),
-        in_specs=[vmem, vmem, vmem, smem, smem, smem, hbm, hbm, hbm],
+        in_specs=[hbm, vmem, vmem, smem, smem, smem, hbm, hbm, hbm],
         out_specs=(vmem, vmem, vmem),
         scratch_shapes=[
+            pltpu.VMEM((T, F, D), BF16),
             pltpu.VMEM((Z, F, T, D), BF16),
             pltpu.VMEM((D, W // 4 * 3), BF16),
             pltpu.VMEM((D, W // 4), BF16),
@@ -433,12 +468,14 @@
             pltpu.VMEM((F, Z * T, W // 4), BF16),
             pltpu.VMEM((3 * F, Z * T, W // 2), BF16),
             pltpu.VMEM((2 * T, W // 4), BF16),
-            pltpu.VMEM((Z, T, D), BF16),
-            pltpu.VMEM((Z, T, D), BF16),
+            pltpu.VMEM((2 * T, D), F32),
+            pltpu.VMEM((Z - 1, T, D), BF16),
+            pltpu.VMEM((Z - 1, T, D), BF16),
             pltpu.VMEM((Z + 1, T, D), BF16),
             pltpu.VMEM((Z + 1, T, D), BF16),
             pltpu.VMEM((T, LAT), BF16),
             pltpu.VMEM((T, LAT), BF16),
+            dma,
             dma((2 * (W // (4 * HD)),)),
             dma,
             dma,
@@ -448,8 +485,8 @@
             dma((2, Z)),
             dma((2, 2, Z)),
             dma((2, 2, Z)),
-            dma((2, Z)),
-            dma((2, Z)),
+            dma((2, 2, Z)),
+            dma((2, 2, Z)),
             dma,
             dma,
         ],
@@ -460,8 +497,8 @@
             flops=2 * Z * T * F * D * W, bytes_accessed=2 * D * W, transcendentals=0
         ),
     )(
-        jnp.swapaxes(hidden, 0, 1),
-        jnp.swapaxes(latent, 0, 1),
+        hidden,
+        latent,
         fresh_noise,
         timesteps,
         queue_slots,
@@ -470,7 +507,14 @@
         attention_weight,
         jnp.transpose(final_weight),
     )
-    return jnp.swapaxes(out, 0, 1), jnp.swapaxes(pred, 0, 1), jnp.swapaxes(queue, 0, 1)
+    return pl.pallas_call(
+        by_token,
+        out_shape=tuple(
+            jax.ShapeDtypeStruct((T, F, x.shape[2]), BF16) for x in (out, pred, queue)
+        ),
+        in_specs=[vmem] * 3,
+        out_specs=(vmem,) * 3,
+    )(out, pred, queue)
 
 
 def solution(mesh):

time: 96.9 us -> 88.5 us (0.913)
  the two profiles are of different devices: /device:TPU:1 before, /device:TPU:31 now
where the time goes in v2:
time: 88.5 us; the launch traced here: 88.4 us
  Pallas kernels  87.7 us (99%)
    pallas_call x1, Pallas kernels, shards(): pl.pallas_call(functools.partial(kernel, Q, Z), out_shape=(jax.ShapeDtype...  85.8 us
    pallas_call x1, Pallas kernels, shards(): pl.pallas_call(by_token, out_shape=tuple((jax.ShapeDtypeStruct((T, F, x.s...  1.96 us

profile of v2, /device:TPU:31, one launch (start us, length us, event | category | flops | bytes accessed | tf_op | source)
XLA Modules:
  0.0 88.4 jit_solution(5597278977688173510)
XLA Ops:
  0.6 85.8 %shard_map.112 = (bf16[2,32,3072]{2,1,0:T(8,128)(2,1)}, bf16[2,32,64]{2,1,0:T(8,128)(2,1)}, bf16[2,32,64]{2,1,0:T(8,128)(2,1)}) custom-call(bf16[32,2,3072]{2,1,0:T(2,128)(2,1)} %hid_hbm.1, bf16[32,2,64]{2,1,0:T(2,128)(2,1)} %lat.1, bf16[32,64]{1,0:T(8,128)(2,1)} %fresh.1, s32[2]{0:T(128)} %steps.1, s32[64]{0:T(128)} %slots.1, s32[64]{0:T(128)} %wins.1, ...), custom_call_target="tpu_custom_call" | custom-call | flops 4831838208 | bytes 9437184 | tf_op jit(solution)/shard_map/pallas_call | solution.py:449
  86.4 2.0 %shard_map.113 = (bf16[32,2,3072]{2,1,0:T(2,128)(2,1)}, bf16[32,2,64]{2,1,0:T(2,128)(2,1)}, bf16[32,2,64]{2,1,0:T(2,128)(2,1)}) custom-call(bf16[2,32,3072]{2,1,0:T(8,128)(2,1)} %get-tuple-element.6.refs_0_, bf16[2,32,64]{2,1,0:T(8,128)(2,1)} %get-tuple-element.7.refs_1_, bf16[2,32,64]{2,1,0:T(8,128)(2,1)} %get-tuple-element.8.refs_2_), custom_call_target="tpu_custom_call" | custom-call | tf_op jit(solution)/shard_map/pallas_call | solution.py:510

commit v3 on v2

--- a/solution.py
+++ b/solution.py
@@ -22,29 +22,43 @@
 NT = (((1,), (1,)), ((), ()))
 
 
+def table(n, values):
+    result = values[0]
+    for k in range(1, len(values)):
+        if values[k] != values[k - 1]:
+            result = result + (values[k] - values[k - 1]) * ((n + len(values) - k) // len(values))
+    return result
+
+
 def kernel(
     Q,
     Z,
     hid_hbm,
-    lat,
-    fresh,
-    steps,
-    slots,
-    wins,
+    lat_hbm,
+    fresh_hbm,
+    steps_hbm,
+    slots_hbm,
+    wins_hbm,
     mw_hbm,
     w_hbm,
     fw_hbm,
     out,
     pred,
     queue,
-    raw,
+    lat,
+    fresh,
+    steps,
+    slots,
+    wins,
     xs,
+    own,
     wqkv,
     wout,
     mw,
     fw,
     part,
     mod,
+    pattern,
     norm,
     qb,
     kv,
@@ -56,7 +70,7 @@
     in_l,
     upd,
     got,
-    hid_sem,
+    small_sem,
     w_sem,
     mw_sem,
     fw_sem,
@@ -111,36 +125,54 @@
         pl.semaphore_signal(barrier, inc=1, device_id=(other, z), device_id_type=MESH)
 
     weights = weight_copies()
-    hid_copy = pltpu.make_async_copy(hid_hbm, raw, hid_sem)
+    small = [
+        pltpu.make_async_copy(src, dst, small_sem.at[i])
+        for i, (src, dst) in enumerate(
+            (
+                (steps_hbm, steps),
+                (slots_hbm, slots),
+                (wins_hbm, wins),
+                (lat_hbm, lat),
+                (fresh_hbm, fresh),
+                (hid_hbm, xs.at[z]),
+            )
+        )
+    ]
     mw_copy = pltpu.make_async_copy(mw_hbm, mw, mw_sem)
     fw_copy = pltpu.make_async_copy(fw_hbm, fw, fw_sem)
-    hid_copy.start()
+    small[0].start()
     mw_copy.start()
-    for copy in weights:
-        copy.start()
-    fw_copy.start()
-
-    def gather_copy(way, u, src, chunk, frame):
+    half = T // 2
+
+    def piece(chunk, part_of):
+        return xs.at[chunk, pl.ds(part_of * half, half)]
+
+    def gather_copy(way, u, src, chunk, part_of):
         return pltpu.make_async_remote_copy(
             src_ref=src,
-            dst_ref=xs.at[chunk, frame],
+            dst_ref=piece(chunk, part_of),
             send_sem=ag_send.at[way, u],
             recv_sem=ag_recv.at[way, u],
             device_id=(q, z_right if way == 0 else z_left),
             device_id_type=MESH,
         )
 
-    for slot in (0, 1):
-        in_r[slot] = jnp.zeros((T, D), BF16)
-        in_l[slot] = jnp.zeros((T, D), BF16)
-
+    def own_copies(u):
+        for way in (0, 1):
+            part_of = u - 1 if way == 0 else 2 - u
+            gather_copy(way, u, hid_hbm.at[pl.ds(part_of * half, half)], z, part_of).start()
+
+    pl.semaphore_wait(barrier, Z + 1)
+    own_copies(1)
+
+    small[0].wait()
     rows = lax.broadcasted_iota(jnp.int32, (8, FREQ), 0)
     lanes = lax.broadcasted_iota(jnp.int32, (8, FREQ), 1)
-    half = FREQ // 2
-    ladder = jnp.exp(lax.rem(lanes, half).astype(F32) * (-math.log(10000.0) / half))
+    waves = FREQ // 2
+    ladder = jnp.exp(lax.rem(lanes, waves).astype(F32) * (-math.log(10000.0) / waves))
     ids = jnp.where(lax.rem(rows, 2) == 0, steps[0], steps[1])
     angles = ids.astype(F32) * ladder
-    freq = jnp.where(lanes < half, jnp.cos(angles), jnp.sin(angles))
+    freq = jnp.where(lanes < waves, jnp.cos(angles), jnp.sin(angles))
     temb = (freq / (1.0 + jnp.exp(-freq))).astype(BF16)
     mw_copy.wait()
     rows = lax.broadcasted_iota(jnp.int32, (8, MP), 0)
@@ -157,64 +189,81 @@
             device_id_type=MESH,
         )
 
-    hid_copy.wait()
-    rows = lax.broadcasted_iota(jnp.int32, (F * T, F * T), 0)
-    cols = lax.broadcasted_iota(jnp.int32, (F * T, F * T), 1)
-    pick = (cols == F * lax.rem(rows, T) + lax.div(rows, T)).astype(BF16)
-    by_frame = jnp.dot(pick, raw[...].reshape(F * T, D), preferred_element_type=F32).astype(BF16)
-    for f in range(F):
-        xs[z, f] = by_frame[f * T : (f + 1) * T]
-
-    pl.semaphore_wait(barrier, Z + 1)
     for k in range(1, Z):
         mod_copy(k, z).start()
-    for u in (1, 2):
-        gather_copy(0, u, xs.at[z, u - 1], z, u - 1).start()
-        gather_copy(1, u, xs.at[z, 2 - u], z, 2 - u).start()
+    own_copies(2)
+    for copy in small[1:] + weights + [fw_copy]:
+        copy.start()
     mod[:, pl.ds(pl.multiple_of(z * MP, MP), MP)] = part[...]
-
-    def normalise(chunk, frame, base):
-        scale = 1.0 + mod[pl.ds(2 + frame, 1), :]
-        shift = mod[pl.ds(frame, 1), :]
-        for r in range(0, T, 16):
-            x = xs[chunk, frame, r : r + 16, :].astype(F32)
+    in_r[0] = jnp.zeros((T, D), BF16)
+    in_l[0] = jnp.zeros((T, D), BF16)
+
+    def choice(rows_count, column_of):
+        rows = lax.broadcasted_iota(jnp.int32, (rows_count, rows_count), 0)
+        cols = lax.broadcasted_iota(jnp.int32, (rows_count, rows_count), 1)
+        return (cols == column_of(rows)).astype(BF16)
+
+    for copy in small[1:]:
+        copy.wait()
+    by_frame = choice(F * T, lambda r: F * lax.rem(r, T) + lax.div(r, T))
+    own_rows = jnp.dot(by_frame, xs[z].reshape(F * T, D), preferred_element_type=F32).astype(BF16)
+    for f in range(F):
+        own[f] = own_rows[f * T : (f + 1) * T]
+
+    def pass_on(u):
+        places = gather_place(u)
+        for way in (0, 1):
+            chunk, part_of = places[way]
+            gather_copy(way, u, piece(chunk, part_of), chunk, part_of).wait_recv()
+
+            @pl.when(u + 2 <= Z - 1)
+            def _():
+                gather_copy(way, u + 2, piece(chunk, part_of), chunk, part_of).start()
+
+    def gather_place(u):
+        step = (u + 1) // 2
+        left = (lax.rem(z + Z - step, Z), lax.rem(u + 1, 2))
+        right = (lax.rem(z + step, Z), lax.rem(u, 2))
+        return left, right
+
+    pass_on(1)
+    for k in range(1, Z):
+        mod_copy(k, lax.rem(z + Z - k, Z)).wait_recv()
+    rows = lax.broadcasted_iota(jnp.int32, (8, D), 0)
+    for p in (0, 1):
+        pattern[p] = jnp.where(
+            lax.rem(rows, 2) == 0, mod[2 * p : 2 * p + 1, :], mod[2 * p + 1 : 2 * p + 2, :]
+        ) + float(p)
+    for copy in weights:
+        copy.wait()
+
+    def normalise(chunk, part_of, base):
+        for r in range(0, half, 8):
+            x = xs[chunk, pl.ds(part_of * half + r, 8)].reshape(16, D).astype(F32)
             centred = x - jnp.sum(x, axis=1, keepdims=True) * (1.0 / D)
             variance = jnp.sum(centred * centred, axis=1, keepdims=True) * (1.0 / D)
-            y = centred * lax.rsqrt(variance + LN_EPS) * scale + shift
-            norm[base + r : base + r + 16, :] = y.astype(BF16)
-
-    def halo_copy(side, u, i, chunk, frame):
-        rows_here = pl.ds(pl.multiple_of(chunk * T, T), T)
+            y = (centred * lax.rsqrt(variance + LN_EPS)).reshape(2, 8, D)
+            y = y * pattern[1][None] + pattern[0][None]
+            norm[base + F * r : base + F * r + 16, :] = y.reshape(16, D).astype(BF16)
+
+    def token_rows(chunk, part_of):
+        return pl.ds(pl.multiple_of(chunk * T + part_of * half, half), half)
+
+    def halo_copy(side, u, i, chunk, part_of):
+        rows_here = token_rows(chunk, part_of)
         return pltpu.make_async_remote_copy(
-            src_ref=kv.at[F + frame, rows_here],
-            dst_ref=kv.at[frame + (0 if side == 0 else 2 * F), rows_here],
+            src_ref=kv.at[pl.ds(F, F), rows_here],
+            dst_ref=kv.at[pl.ds(0 if side == 0 else 2 * F, F), rows_here],
             send_sem=halo_send.at[side, i, u],
             recv_sem=halo_recv.at[side, i, u],
             device_id=(q_right if side == 0 else q_left, z),
             device_id_type=MESH,
         )
 
-    def gather_place(u):
-        step = (u + 1) // 2
-        left = (lax.rem(z + Z - step, Z), lax.rem(u + 1, 2))
-        right = (lax.rem(z + step, Z), lax.rem(u, 2))
-        return left, right
-
-    def pass_on(u):
-        places = gather_place(u)
-        for way in (0, 1):
-            chunk, frame = places[way]
-            gather_copy(way, u, xs.at[chunk, frame], chunk, frame).wait_recv()
-
-            @pl.when(u + 2 <= Z - 1)
-            def _():
-                gather_copy(way, u + 2, xs.at[chunk, frame], chunk, frame).start()
-
-    pass_on(1)
-    for k in range(1, Z):
-        mod_copy(k, lax.rem(z + Z - k, Z)).wait_recv()
-    for copy in weights:
-        copy.wait()
+    split = choice(
+        2 * T,
+        lambda r: lax.rem(lax.div(r, half), 2) * T + F * lax.rem(r, half) + lax.div(r, T),
+    )
 
     def gather_unit(u, carry):
         places = gather_place(u)
@@ -222,19 +271,21 @@
 
         for way in (0, 1):
             normalise(*places[way], way * T)
-        projected = jnp.dot(norm[...], wqkv[...], preferred_element_type=F32).astype(BF16)
+        mixed_rows = jnp.dot(norm[...], wqkv[...], preferred_element_type=F32).astype(BF16)
+        projected = jnp.dot(split, mixed_rows, preferred_element_type=F32).astype(BF16)
         for way in (0, 1):
-            chunk, frame = places[way]
-            rows_here = pl.ds(pl.multiple_of(chunk * T, T), T)
-            block = projected[way * T : (way + 1) * T]
-            for h in range(LH):
-                at = h * 3 * HD
-                qb[frame, rows_here, h * HD : (h + 1) * HD] = block[:, at : at + HD]
-                kv[F + frame, rows_here, h * 2 * HD : (h + 1) * 2 * HD] = block[
-                    :, at + HD : at + 3 * HD
-                ]
+            rows_here = token_rows(*places[way])
+            for f in range(F):
+                at_row = f * T + way * half
+                block = projected[at_row : at_row + half]
+                for h in range(LH):
+                    at = h * 3 * HD
+                    qb[f, rows_here, h * HD : (h + 1) * HD] = block[:, at : at + HD]
+                    kv[F + f, rows_here, h * 2 * HD : (h + 1) * 2 * HD] = block[
+                        :, at + HD : at + 3 * HD
+                    ]
             for side in (0, 1):
-                halo_copy(side, u, way, chunk, frame).start()
+                halo_copy(side, u, way, *places[way]).start()
         return carry
 
     lax.fori_loop(0, Z, gather_unit, 0)
@@ -293,14 +344,12 @@
             results.append(mixed / total)
         return results
 
-    half = T // 2
-
     def scatter_copy(way, n, part_of):
         src, dst = (sent_r, in_r) if way == 0 else (sent_l, in_l)
         rows_here = pl.ds(part_of * half, half)
         return pltpu.make_async_remote_copy(
             src_ref=src.at[n - 1, rows_here],
-            dst_ref=dst.at[n + 1, rows_here],
+            dst_ref=dst.at[n, rows_here],
             send_sem=rs_send.at[way, part_of, n],
             recv_sem=rs_recv.at[way, part_of, n],
             device_id=(q, z_right if way == 0 else z_left),
@@ -308,15 +357,19 @@
         )
 
     def scatter_unit(n, carry):
-        step = Z // 2 - n // 2
-        late = n // (Z - 2) - n // Z
-        right = (lax.rem(z + step, Z), lax.rem(n + 1 + late, 2))
-        left = (lax.rem(z + Z - step, Z), lax.rem(n, 2))
+        right_step = table(n, (0, 3, 4, 2, 3, 2, 1, 1, 0))
+        left_step = table(n, (0, 3, 4, 2, 3, 1, 2, 1, 0))
+        right = (lax.rem(z + right_step, Z), table(n, (1, 1, 0, 1, 0, 0, 0, 1, 1)))
+        left = (lax.rem(z + Z - left_step, Z), table(n, (0, 0, 1, 0, 1, 0, 1, 1, 0)))
         spread = [spatial(*right), spatial(*left)]
 
         @pl.when(n == 1)
         def _():
-            lax.fori_loop(0, Z, halo_wait, 0)
+            lax.fori_loop(0, Z - 1, halo_wait, 0)
+
+        @pl.when(n == 2)
+        def _():
+            halo_wait(Z - 1, 0)
 
         along = [temporal(*right), temporal(*left)]
         for i in (0, 1):
@@ -332,7 +385,10 @@
 
         @pl.when(n <= Z - 1)
         def _():
-            needs = (n - 2 + late * (2 * Z - 3 - 2 * n), n - 2)
+            needs = (
+                table(n, (0, 0, 0, 1, 2, 4, 5, 3, 0)),
+                table(n, (0, 0, 0, 1, 2, 3, 4, 6, 0)),
+            )
             for part_of in (0, 1):
                 for way, (sent, arrived) in enumerate(((sent_r, in_r), (sent_l, in_l))):
                     need = needs[way]
@@ -344,7 +400,7 @@
                     mine = way * T + part_of * half
                     rows_here = slice(part_of * half, (part_of + 1) * half)
                     sent[n - 1, rows_here, :] = (
-                        share[mine : mine + half, :] + arrived[need + 1, rows_here, :].astype(F32)
+                        share[mine : mine + half, :] + arrived[need, rows_here, :].astype(F32)
                     ).astype(BF16)
                     scatter_copy(way, n, part_of).start()
 
@@ -371,18 +427,19 @@
         device_id=(q_left, z),
         device_id_type=MESH,
     )
+    last = ((6, 5), (7, 7))
     for f in range(F):
         for way in (0, 1):
             for part_of in (0, 1):
-                scatter_copy(way, Z - 2 + f, part_of).wait_recv()
+                scatter_copy(way, last[f][way], part_of).wait_recv()
         mine = (1 - f) * T
         total = (
             share[mine : mine + T, :]
-            + in_r[Z - 1 + f].astype(F32)
-            + in_l[Z - 1 + f].astype(F32)
+            + in_r[last[f][0]].astype(F32)
+            + in_l[last[f][1]].astype(F32)
         )
         gate = mod[4 + f : 5 + f, :]
-        block = (xs[z, f].astype(F32) + gate * total).astype(BF16)
+        block = (own[f].astype(F32) + gate * total).astype(BF16)
         out[f] = block
         noise = lax.dot_general(block, fw[...], NT, preferred_element_type=F32)
         pred[f] = noise.astype(BF16)
@@ -404,16 +461,16 @@
     def drain(u, carry):
         places = gather_place(u)
         for way in (0, 1):
-            chunk, frame = places[way]
+            chunk, part_of = places[way]
 
             @pl.when(u >= 1)
             def _():
-                gather_copy(way, u, xs.at[chunk, frame], chunk, frame).wait_send()
-                for part_of in (0, 1):
-                    scatter_copy(way, u, part_of).wait_send()
+                gather_copy(way, u, piece(chunk, part_of), chunk, part_of).wait_send()
+                for rows_part in (0, 1):
+                    scatter_copy(way, u, rows_part).wait_send()
 
             for side in (0, 1):
-                halo_copy(side, u, way, chunk, frame).wait_send()
+                halo_copy(side, u, way, chunk, part_of).wait_send()
         return carry
 
     lax.fori_loop(0, Z, drain, 0)
@@ -443,7 +500,6 @@
     W = attention_weight.shape[1]
     MP = mod_weight.shape[2]
     vmem = pl.BlockSpec(memory_space=pltpu.VMEM)
-    smem = pl.BlockSpec(memory_space=pltpu.SMEM)
     hbm = pl.BlockSpec(memory_space=pltpu.HBM)
     dma = pltpu.SemaphoreType.DMA
     out, pred, queue = pl.pallas_call(
@@ -453,17 +509,23 @@
             jax.ShapeDtypeStruct((F, T, LAT), BF16),
             jax.ShapeDtypeStruct((F, T, LAT), BF16),
         ),
-        in_specs=[hbm, vmem, vmem, smem, smem, smem, hbm, hbm, hbm],
+        in_specs=[hbm] * 9,
         out_specs=(vmem, vmem, vmem),
         scratch_shapes=[
-            pltpu.VMEM((T, F, D), BF16),
-            pltpu.VMEM((Z, F, T, D), BF16),
+            pltpu.VMEM(latent.shape, BF16),
+            pltpu.VMEM(fresh_noise.shape, BF16),
+            pltpu.SMEM(timesteps.shape, jnp.int32),
+            pltpu.SMEM(queue_slots.shape, jnp.int32),
+            pltpu.SMEM(windows.shape, jnp.int32),
+            pltpu.VMEM((Z, T, F, D), BF16),
+            pltpu.VMEM((F, T, D), BF16),
             pltpu.VMEM((D, W // 4 * 3), BF16),
             pltpu.VMEM((D, W // 4), BF16),
             pltpu.VMEM(mod_weight.shape, BF16),
             pltpu.VMEM((LAT, D), BF16),
             pltpu.VMEM((8, MP), F32),
             pltpu.VMEM((8, D), F32),
+            pltpu.VMEM((2, 8, D), F32),
             pltpu.VMEM((2 * T, D), BF16),
             pltpu.VMEM((F, Z * T, W // 4), BF16),
             pltpu.VMEM((3 * F, Z * T, W // 2), BF16),
@@ -471,11 +533,11 @@
             pltpu.VMEM((2 * T, D), F32),
             pltpu.VMEM((Z - 1, T, D), BF16),
             pltpu.VMEM((Z - 1, T, D), BF16),
-            pltpu.VMEM((Z + 1, T, D), BF16),
-            pltpu.VMEM((Z + 1, T, D), BF16),
+            pltpu.VMEM((Z, T, D), BF16),
+            pltpu.VMEM((Z, T, D), BF16),
             pltpu.VMEM((T, LAT), BF16),
             pltpu.VMEM((T, LAT), BF16),
-            dma,
+            dma((6,)),
             dma((2 * (W // (4 * HD)),)),
             dma,
             dma,

time: 88.5 us -> 86.2 us (0.974)
  the two profiles are of different devices: /device:TPU:31 before, /device:TPU:1 now
where the time goes in v3:
time: 86.2 us; the launch traced here: 86 us
  Pallas kernels  85.3 us (99%)
    pallas_call x1, Pallas kernels, shards(): pl.pallas_call(functools.partial(kernel, Q, Z), out_shape=(jax.ShapeDtype...  83.4 us
    pallas_call x1, Pallas kernels, shards(): pl.pallas_call(by_token, out_shape=tuple((jax.ShapeDtypeStruct((T, F, x.s...  1.96 us

profile of v3, /device:TPU:1, one launch (start us, length us, event | category | flops | bytes accessed | tf_op | source)
XLA Modules:
  0.0 86.0 jit_solution(3422193446060378627)
XLA Ops:
  0.6 83.4 %shard_map.112 = (bf16[2,32,3072]{2,1,0:T(8,128)(2,1)}, bf16[2,32,64]{2,1,0:T(8,128)(2,1)}, bf16[2,32,64]{2,1,0:T(8,128)(2,1)}) custom-call(bf16[32,2,3072]{2,1,0:T(2,128)(2,1)} %hid_hbm.1, bf16[32,2,64]{2,1,0:T(2,128)(2,1)} %lat_hbm.1, bf16[32,64]{1,0:T(8,128)(2,1)} %fresh_hbm.1, s32[2]{0:T(128)} %steps_hbm.1, s32[64]{0:T(128)} %slots_hbm.1, s32[64]{0:T(128)} %wins_hbm.1, ...), custom_call_target="tpu_custom_call" | custom-call | flops 4831838208 | bytes 9437184 | tf_op jit(solution)/shard_map/pallas_call | solution.py:505
  84.0 2.0 %shard_map.113 = (bf16[32,2,3072]{2,1,0:T(2,128)(2,1)}, bf16[32,2,64]{2,1,0:T(2,128)(2,1)}, bf16[32,2,64]{2,1,0:T(2,128)(2,1)}) custom-call(bf16[2,32,3072]{2,1,0:T(8,128)(2,1)} %get-tuple-element.6.refs_0_, bf16[2,32,64]{2,1,0:T(8,128)(2,1)} %get-tuple-element.7.refs_1_, bf16[2,32,64]{2,1,0:T(8,128)(2,1)} %get-tuple-element.8.refs_2_), custom_call_target="tpu_custom_call" | custom-call | tf_op jit(solution)/shard_map/pallas_call | solution.py:572

commit v4 on v3

--- a/solution.py
+++ b/solution.py
@@ -58,6 +58,8 @@
     fw,
     part,
     mod,
+    gate_part,
+    gates_all,
     pattern,
     norm,
     qb,
@@ -76,6 +78,8 @@
     fw_sem,
     mod_send,
     mod_recv,
+    gate_send,
+    gate_recv,
     ag_send,
     ag_recv,
     halo_send,
@@ -175,9 +179,12 @@
     freq = jnp.where(lanes < waves, jnp.cos(angles), jnp.sin(angles))
     temb = (freq / (1.0 + jnp.exp(-freq))).astype(BF16)
     mw_copy.wait()
+    maps = [jnp.dot(temb, mw[p], preferred_element_type=F32) for p in range(3)]
     rows = lax.broadcasted_iota(jnp.int32, (8, MP), 0)
-    maps = [jnp.dot(temb, mw[p], preferred_element_type=F32) for p in range(3)]
-    part[...] = jnp.where(rows < 2, maps[0], jnp.where(rows < 4, maps[1], maps[2]))
+    pairs = jnp.where(rows < 2, maps[0], maps[1])
+    my_columns = pl.ds(pl.multiple_of(z * MP, MP), MP)
+    part[...] = pairs[: 2 * F]
+    gate_part[...] = maps[2][:F]
 
     def mod_copy(k, owner):
         return pltpu.make_async_remote_copy(
@@ -189,12 +196,23 @@
             device_id_type=MESH,
         )
 
+    def gate_copy(k, owner):
+        return pltpu.make_async_remote_copy(
+            src_ref=gate_part,
+            dst_ref=gates_all.at[:, pl.ds(pl.multiple_of(owner * MP, MP), MP)],
+            send_sem=gate_send.at[k],
+            recv_sem=gate_recv.at[k],
+            device_id=(q, lax.rem(z + k, Z)),
+            device_id_type=MESH,
+        )
+
     for k in range(1, Z):
         mod_copy(k, z).start()
     own_copies(2)
     for copy in small[1:] + weights + [fw_copy]:
         copy.start()
-    mod[:, pl.ds(pl.multiple_of(z * MP, MP), MP)] = part[...]
+    mod[:, my_columns] = part[...]
+    gates_all[:, my_columns] = gate_part[...]
     in_r[0] = jnp.zeros((T, D), BF16)
     in_l[0] = jnp.zeros((T, D), BF16)
 
@@ -264,6 +282,12 @@
         2 * T,
         lambda r: lax.rem(lax.div(r, half), 2) * T + F * lax.rem(r, half) + lax.div(r, T),
     )
+
+    def halo_wait(u):
+        places = gather_place(u)
+        for way in (0, 1):
+            for side in (0, 1):
+                halo_copy(side, u, way, *places[way]).wait_recv()
 
     def gather_unit(u, carry):
         places = gather_place(u)
@@ -286,30 +310,42 @@
                     ]
             for side in (0, 1):
                 halo_copy(side, u, way, *places[way]).start()
+
+        @pl.when(u >= 2)
+        def _():
+            halo_wait(u - 2)
+
         return carry
 
     lax.fori_loop(0, Z, gather_unit, 0)
-
-    def halo_wait(u, carry):
-        places = gather_place(u)
-        for way in (0, 1):
-            for side in (0, 1):
-                halo_copy(side, u, way, *places[way]).wait_recv()
-        return carry
-
-    def spatial(chunk, frame):
-        rows_here = pl.ds(pl.multiple_of(chunk * T, T), T)
-        results = []
-        for h in range(LH):
-            queries = qb[frame, rows_here, h * HD : (h + 1) * HD]
-            keys = kv[F + frame, :, h * 2 * HD : h * 2 * HD + HD]
-            values = kv[F + frame, :, h * 2 * HD + HD : (h + 1) * 2 * HD]
-            scores = lax.dot_general(queries, keys, NT, preferred_element_type=F32) * factor
-            expo = jnp.exp(scores - jnp.max(scores, axis=1, keepdims=True))
-            total = jnp.sum(expo, axis=1, keepdims=True)
-            mixed = jnp.dot(expo.astype(BF16), values, preferred_element_type=F32)
-            results.append(mixed / total)
-        return results
+    for k in range(1, Z):
+        gate_copy(k, z).start()
+
+    def spatial(pieces):
+        each = [(chunk, frame, h) for chunk, frame in pieces for h in range(LH)]
+        scores = [
+            lax.dot_general(
+                qb[frame, pl.ds(pl.multiple_of(chunk * T, T), T), h * HD : (h + 1) * HD],
+                kv[F + frame, :, h * 2 * HD : h * 2 * HD + HD],
+                NT,
+                preferred_element_type=F32,
+            )
+            for chunk, frame, h in each
+        ]
+        scores = [score * factor for score in scores]
+        peaks = [jnp.max(score, axis=1, keepdims=True) for score in scores]
+        expos = [jnp.exp(score - peak) for score, peak in zip(scores, peaks)]
+        totals = [jnp.sum(expo, axis=1, keepdims=True) for expo in expos]
+        mixed = [
+            jnp.dot(
+                expo.astype(BF16),
+                kv[F + frame, :, h * 2 * HD + HD : (h + 1) * 2 * HD],
+                preferred_element_type=F32,
+            )
+            for expo, (chunk, frame, h) in zip(expos, each)
+        ]
+        results = [m / total for m, total in zip(mixed, totals)]
+        return [results[:LH], results[LH:]]
 
     def temporal(chunk, frame):
         rows_here = pl.ds(pl.multiple_of(chunk * T, T), T)
@@ -361,15 +397,15 @@
         left_step = table(n, (0, 3, 4, 2, 3, 1, 2, 1, 0))
         right = (lax.rem(z + right_step, Z), table(n, (1, 1, 0, 1, 0, 0, 0, 1, 1)))
         left = (lax.rem(z + Z - left_step, Z), table(n, (0, 0, 1, 0, 1, 0, 1, 1, 0)))
-        spread = [spatial(*right), spatial(*left)]
+        spread = spatial([right, left])
 
         @pl.when(n == 1)
         def _():
-            lax.fori_loop(0, Z - 1, halo_wait, 0)
+            halo_wait(Z - 2)
 
         @pl.when(n == 2)
         def _():
-            halo_wait(Z - 1, 0)
+            halo_wait(Z - 1)
 
         along = [temporal(*right), temporal(*left)]
         for i in (0, 1):
@@ -404,11 +440,32 @@
                     ).astype(BF16)
                     scatter_copy(way, n, part_of).start()
 
+        @pl.when(n >= 2)
+        def _():
+            u = n - 1
+            places = gather_place(u)
+            for way in (0, 1):
+                gather_copy(way, u, piece(*places[way]), *places[way]).wait_send()
+
+        @pl.when(n >= 3)
+        def _():
+            for way in (0, 1):
+                for part_of in (0, 1):
+                    scatter_copy(way, n - 2, part_of).wait_send()
+
+        halo_places = gather_place(n - 1)
+        for way in (0, 1):
+            for side in (0, 1):
+                halo_copy(side, n - 1, way, *halo_places[way]).wait_send()
         return carry
 
     lax.fori_loop(1, Z + 1, scatter_unit, 0)
 
     fw_copy.wait()
+    for k in range(1, Z):
+        gate_copy(k, lax.rem(z + Z - k, Z)).wait_recv()
+        gate_copy(k, z).wait_send()
+        mod_copy(k, z).wait_send()
     horizon = STRIDE * (FRAMES + 1)
     LAT = lat.shape[2]
 
@@ -438,7 +495,7 @@
             + in_r[last[f][0]].astype(F32)
             + in_l[last[f][1]].astype(F32)
         )
-        gate = mod[4 + f : 5 + f, :]
+        gate = gates_all[f : f + 1, :]
         block = (own[f].astype(F32) + gate * total).astype(BF16)
         out[f] = block
         noise = lax.dot_general(block, fw[...], NT, preferred_element_type=F32)
@@ -455,25 +512,9 @@
     queue[F - 1] = jnp.where(q == Q - 1, fresh[...], got[...])
 
     edge.wait_send()
-    for k in range(1, Z):
-        mod_copy(k, z).wait_send()
-
-    def drain(u, carry):
-        places = gather_place(u)
-        for way in (0, 1):
-            chunk, part_of = places[way]
-
-            @pl.when(u >= 1)
-            def _():
-                gather_copy(way, u, piece(chunk, part_of), chunk, part_of).wait_send()
-                for rows_part in (0, 1):
-                    scatter_copy(way, u, rows_part).wait_send()
-
-            for side in (0, 1):
-                halo_copy(side, u, way, chunk, part_of).wait_send()
-        return carry
-
-    lax.fori_loop(0, Z, drain, 0)
+    for way in (0, 1):
+        for part_of in (0, 1):
+            scatter_copy(way, Z - 1, part_of).wait_send()
 
 
 def by_token(*refs):
@@ -523,8 +564,10 @@
             pltpu.VMEM((D, W // 4), BF16),
             pltpu.VMEM(mod_weight.shape, BF16),
             pltpu.VMEM((LAT, D), BF16),
-            pltpu.VMEM((8, MP), F32),
-            pltpu.VMEM((8, D), F32),
+            pltpu.VMEM((2 * F, MP), F32),
+            pltpu.VMEM((2 * F, D), F32),
+            pltpu.VMEM((F, MP), F32),
+            pltpu.VMEM((F, D), F32),
             pltpu.VMEM((2, 8, D), F32),
             pltpu.VMEM((2 * T, D), BF16),
             pltpu.VMEM((F, Z * T, W // 4), BF16),
@@ -541,6 +584,8 @@
             dma((2 * (W // (4 * HD)),)),
             dma,
             dma,
+            dma((Z,)),
+            dma((Z,)),
             dma((Z,)),
             dma((Z,)),
             dma((2, Z)),

time: 86.2 us -> 83.5 us (0.969)
  Pallas kernels: 85.3 us -> 82.7 us
    pallas_call x1, Pallas kernels: 83.4 us -> 80.8 us  [shards(): pl.pallas_call(functools.partial(kernel, Q, Z), out_shape=(jax.ShapeDtype...]
where the time goes in v4:
time: 83.5 us; the launch traced here: 83.4 us
  Pallas kernels  82.7 us (99%)
    pallas_call x1, Pallas kernels, shards(): pl.pallas_call(functools.partial(kernel, Q, Z), out_shape=(jax.ShapeDtype...  80.8 us
    pallas_call x1, Pallas kernels, shards(): pl.pallas_call(by_token, out_shape=tuple((jax.ShapeDtypeStruct((T, F, x.s...  1.96 us

profile of v4, /device:TPU:1, one launch (start us, length us, event | category | flops | bytes accessed | tf_op | source)
XLA Modules:
  0.0 83.4 jit_solution(6884380369319607051)
XLA Ops:
  0.6 80.8 %shard_map.112 = (bf16[2,32,3072]{2,1,0:T(8,128)(2,1)}, bf16[2,32,64]{2,1,0:T(8,128)(2,1)}, bf16[2,32,64]{2,1,0:T(8,128)(2,1)}) custom-call(bf16[32,2,3072]{2,1,0:T(2,128)(2,1)} %hid_hbm.1, bf16[32,2,64]{2,1,0:T(2,128)(2,1)} %lat_hbm.1, bf16[32,64]{1,0:T(8,128)(2,1)} %fresh_hbm.1, s32[2]{0:T(128)} %steps_hbm.1, s32[64]{0:T(128)} %slots_hbm.1, s32[64]{0:T(128)} %wins_hbm.1, ...), custom_call_target="tpu_custom_call" | custom-call | flops 4831838208 | bytes 9437184 | tf_op jit(solution)/shard_map/pallas_call | solution.py:546
  81.4 2.0 %shard_map.113 = (bf16[32,2,3072]{2,1,0:T(2,128)(2,1)}, bf16[32,2,64]{2,1,0:T(2,128)(2,1)}, bf16[32,2,64]{2,1,0:T(2,128)(2,1)}) custom-call(bf16[2,32,3072]{2,1,0:T(8,128)(2,1)} %get-tuple-element.6.refs_0_, bf16[2,32,64]{2,1,0:T(8,128)(2,1)} %get-tuple-element.7.refs_1_, bf16[2,32,64]{2,1,0:T(8,128)(2,1)} %get-tuple-element.8.refs_2_), custom_call_target="tpu_custom_call" | custom-call | tf_op jit(solution)/shard_map/pallas_call | solution.py:617

commit v5 on v4

--- a/solution.py
+++ b/solution.py
@@ -52,8 +52,10 @@
     wins,
     xs,
     own,
-    wqkv,
+    wq,
+    wkv,
     wout,
+    wout_turned,
     mw,
     fw,
     part,
@@ -102,22 +104,15 @@
 
     def weight_copies():
         copies = []
-        for h in range(LH):
-            copies.append(
-                pltpu.make_async_copy(
-                    w_hbm.at[:, pl.ds(h * 4 * HD, 3 * HD)],
-                    wqkv.at[:, pl.ds(h * 3 * HD, 3 * HD)],
-                    w_sem.at[h],
+        for target, first, width in ((wkv, HD, 2 * HD), (wq, 0, HD), (wout, 3 * HD, HD)):
+            for h in range(LH):
+                copies.append(
+                    pltpu.make_async_copy(
+                        w_hbm.at[:, pl.ds(h * 4 * HD + first, width)],
+                        target.at[:, pl.ds(h * width, width)],
+                        w_sem.at[len(copies)],
+                    )
                 )
-            )
-        for h in range(LH):
-            copies.append(
-                pltpu.make_async_copy(
-                    w_hbm.at[:, pl.ds(h * 4 * HD + 3 * HD, HD)],
-                    wout.at[:, pl.ds(h * HD, HD)],
-                    w_sem.at[LH + h],
-                )
-            )
         return copies
 
     barrier = pltpu.get_barrier_semaphore()
@@ -254,6 +249,12 @@
         ) + float(p)
     for copy in weights:
         copy.wait()
+    same = choice(LH * HD, lambda r: r)
+    tile = 512
+    for c in range(0, D, tile):
+        wout_turned[:, c : c + tile] = lax.dot_general(
+            same, wout[c : c + tile, :], NT, preferred_element_type=F32
+        ).astype(BF16)
 
     def normalise(chunk, part_of, base):
         for r in range(0, half, 8):
@@ -289,27 +290,37 @@
             for side in (0, 1):
                 halo_copy(side, u, way, *places[way]).wait_recv()
 
+    def project(weight):
+        mixed_rows = jnp.dot(norm[...], weight[...], preferred_element_type=F32).astype(BF16)
+        return jnp.dot(split, mixed_rows, preferred_element_type=F32).astype(BF16)
+
+    def keep_queries(u):
+        places = gather_place(u)
+        projected = project(wq)
+        for way in (0, 1):
+            rows_here = token_rows(*places[way])
+            for f in range(F):
+                at_row = f * T + way * half
+                qb[f, rows_here, :] = projected[at_row : at_row + half]
+
     def gather_unit(u, carry):
         places = gather_place(u)
         pl.when(u >= 2)(lambda: pass_on(u))
 
         for way in (0, 1):
             normalise(*places[way], way * T)
-        mixed_rows = jnp.dot(norm[...], wqkv[...], preferred_element_type=F32).astype(BF16)
-        projected = jnp.dot(split, mixed_rows, preferred_element_type=F32).astype(BF16)
+        projected = project(wkv)
         for way in (0, 1):
             rows_here = token_rows(*places[way])
             for f in range(F):
                 at_row = f * T + way * half
-                block = projected[at_row : at_row + half]
-                for h in range(LH):
-                    at = h * 3 * HD
-                    qb[f, rows_here, h * HD : (h + 1) * HD] = block[:, at : at + HD]
-                    kv[F + f, rows_here, h * 2 * HD : (h + 1) * 2 * HD] = block[
-                        :, at + HD : at + 3 * HD
-                    ]
+                kv[F + f, rows_here, :] = projected[at_row : at_row + half]
             for side in (0, 1):
                 halo_copy(side, u, way, *places[way]).start()
+
+        @pl.when(u < Z - 1)
+        def _():
+            keep_queries(u)
 
         @pl.when(u >= 2)
         def _():
@@ -392,18 +403,45 @@
             device_id_type=MESH,
         )
 
-    def scatter_unit(n, carry):
-        right_step = table(n, (0, 3, 4, 2, 3, 2, 1, 1, 0))
-        left_step = table(n, (0, 3, 4, 2, 3, 1, 2, 1, 0))
-        right = (lax.rem(z + right_step, Z), table(n, (1, 1, 0, 1, 0, 0, 0, 1, 1)))
-        left = (lax.rem(z + Z - left_step, Z), table(n, (0, 0, 1, 0, 1, 0, 1, 1, 0)))
+    def drain(u, carry):
+        places = gather_place(u)
+        for way in (0, 1):
+
+            @pl.when(u >= 1)
+            def _():
+                gather_copy(way, u, piece(*places[way]), *places[way]).wait_send()
+
+            for side in (0, 1):
+                halo_copy(side, u, way, *places[way]).wait_send()
+        return carry
+
+    def sent_off(n, carry):
+        for way in (0, 1):
+            for part_of in (0, 1):
+                scatter_copy(way, n, part_of).wait_send()
+        return carry
+
+    own_turn = Z // 2
+
+    def scatter_unit(m, carry):
+        n = table(m, (0, 1, 2, 3, 0, 4, 5, 6, 7))
+        right_step = table(m, (0, 3, 4, 2, 0, 3, 2, 1, 1))
+        left_step = table(m, (0, 3, 4, 2, 0, 3, 1, 2, 1))
+        right = (lax.rem(z + right_step, Z), table(m, (1, 1, 0, 1, 1, 0, 0, 0, 1)))
+        left = (lax.rem(z + Z - left_step, Z), table(m, (0, 0, 1, 0, 0, 1, 0, 1, 1)))
+        place = table(m, (0, 0, 0, 0, 1, 0, 0, 0, 0))
+
+        @pl.when(m == 2)
+        def _():
+            keep_queries(Z - 1)
+
         spread = spatial([right, left])
 
-        @pl.when(n == 1)
+        @pl.when(m == 1)
         def _():
             halo_wait(Z - 2)
 
-        @pl.when(n == 2)
+        @pl.when(m == 2)
         def _():
             halo_wait(Z - 1)
 
@@ -413,54 +451,42 @@
                 hd[i * T : (i + 1) * T, h * HD : (h + 1) * HD] = (
                     spread[i][h] + along[i][h]
                 ).astype(BF16)
-        tile = 512
         for c in range(0, D, tile):
-            share[:, c : c + tile] = lax.dot_general(
-                hd[...], wout[c : c + tile, :], NT, preferred_element_type=F32
+            share[place, :, c : c + tile] = jnp.dot(
+                hd[...], wout_turned[:, c : c + tile], preferred_element_type=F32
             )
 
-        @pl.when(n <= Z - 1)
+        @pl.when(m != own_turn)
         def _():
             needs = (
-                table(n, (0, 0, 0, 1, 2, 4, 5, 3, 0)),
-                table(n, (0, 0, 0, 1, 2, 3, 4, 6, 0)),
+                table(m, (0, 0, 0, 1, 0, 2, 4, 5, 3)),
+                table(m, (0, 0, 0, 1, 0, 2, 3, 4, 6)),
             )
             for part_of in (0, 1):
                 for way, (sent, arrived) in enumerate(((sent_r, in_r), (sent_l, in_l))):
                     need = needs[way]
 
-                    @pl.when(n >= 3)
+                    @pl.when(m >= 3)
                     def _():
                         scatter_copy(way, need, part_of).wait_recv()
 
                     mine = way * T + part_of * half
                     rows_here = slice(part_of * half, (part_of + 1) * half)
                     sent[n - 1, rows_here, :] = (
-                        share[mine : mine + half, :] + arrived[need, rows_here, :].astype(F32)
+                        share[0, mine : mine + half, :]
+                        + arrived[need, rows_here, :].astype(F32)
                     ).astype(BF16)
                     scatter_copy(way, n, part_of).start()
 
-        @pl.when(n >= 2)
+        @pl.when(m == own_turn)
         def _():
-            u = n - 1
-            places = gather_place(u)
-            for way in (0, 1):
-                gather_copy(way, u, piece(*places[way]), *places[way]).wait_send()
-
-        @pl.when(n >= 3)
-        def _():
-            for way in (0, 1):
-                for part_of in (0, 1):
-                    scatter_copy(way, n - 2, part_of).wait_send()
-
-        halo_places = gather_place(n - 1)
-        for way in (0, 1):
-            for side in (0, 1):
-                halo_copy(side, n - 1, way, *halo_places[way]).wait_send()
+            lax.fori_loop(0, Z, drain, 0)
+
         return carry
 
     lax.fori_loop(1, Z + 1, scatter_unit, 0)
 
+    lax.fori_loop(1, Z - 2, sent_off, 0)
     fw_copy.wait()
     for k in range(1, Z):
         gate_copy(k, lax.rem(z + Z - k, Z)).wait_recv()
@@ -491,7 +517,7 @@
                 scatter_copy(way, last[f][way], part_of).wait_recv()
         mine = (1 - f) * T
         total = (
-            share[mine : mine + T, :]
+            share[1, mine : mine + T, :]
             + in_r[last[f][0]].astype(F32)
             + in_l[last[f][1]].astype(F32)
         )
@@ -512,9 +538,7 @@
     queue[F - 1] = jnp.where(q == Q - 1, fresh[...], got[...])
 
     edge.wait_send()
-    for way in (0, 1):
-        for part_of in (0, 1):
-            scatter_copy(way, Z - 1, part_of).wait_send()
+    lax.fori_loop(Z - 2, Z, sent_off, 0)
 
 
 def by_token(*refs):
@@ -560,8 +584,10 @@
             pltpu.SMEM(windows.shape, jnp.int32),
             pltpu.VMEM((Z, T, F, D), BF16),
             pltpu.VMEM((F, T, D), BF16),
-            pltpu.VMEM((D, W // 4 * 3), BF16),
             pltpu.VMEM((D, W // 4), BF16),
+            pltpu.VMEM((D, W // 2), BF16),
+            pltpu.VMEM((D, W // 4), BF16),
+            pltpu.VMEM((W // 4, D), BF16),
             pltpu.VMEM(mod_weight.shape, BF16),
             pltpu.VMEM((LAT, D), BF16),
             pltpu.VMEM((2 * F, MP), F32),
@@ -573,7 +599,7 @@
             pltpu.VMEM((F, Z * T, W // 4), BF16),
             pltpu.VMEM((3 * F, Z * T, W // 2), BF16),
             pltpu.VMEM((2 * T, W // 4), BF16),
-            pltpu.VMEM((2 * T, D), F32),
+            pltpu.VMEM((2, 2 * T, D), F32),
             pltpu.VMEM((Z - 1, T, D), BF16),
             pltpu.VMEM((Z - 1, T, D), BF16),
             pltpu.VMEM((Z, T, D), BF16),
@@ -581,7 +607,7 @@
             pltpu.VMEM((T, LAT), BF16),
             pltpu.VMEM((T, LAT), BF16),
             dma((6,)),
-            dma((2 * (W // (4 * HD)),)),
+            dma((3 * (W // (4 * HD)),)),
             dma,
             dma,
             dma((Z,)),

time: 83.5 us -> 82.5 us (0.988)
  Pallas kernels: 82.7 us -> 81.7 us
    pallas_call x1, Pallas kernels: 80.8 us -> 79.8 us  [shards(): pl.pallas_call(functools.partial(kernel, Q, Z), out_shape=(jax.ShapeDtype...]
where the time goes in v5:
time: 82.5 us; the launch traced here: 82.4 us
  Pallas kernels  81.7 us (99%)
    pallas_call x1, Pallas kernels, shards(): pl.pallas_call(functools.partial(kernel, Q, Z), out_shape=(jax.ShapeDtype...  79.8 us
    pallas_call x1, Pallas kernels, shards(): pl.pallas_call(by_token, out_shape=tuple((jax.ShapeDtypeStruct((T, F, x.s...  1.96 us

profile of v5, /device:TPU:1, one launch (start us, length us, event | category | flops | bytes accessed | tf_op | source)
XLA Modules:
  0.0 82.4 jit_solution(6193210257303539719)
XLA Ops:
  0.6 79.8 %shard_map.112 = (bf16[2,32,3072]{2,1,0:T(8,128)(2,1)}, bf16[2,32,64]{2,1,0:T(8,128)(2,1)}, bf16[2,32,64]{2,1,0:T(8,128)(2,1)}) custom-call(bf16[32,2,3072]{2,1,0:T(2,128)(2,1)} %hid_hbm.1, bf16[32,2,64]{2,1,0:T(2,128)(2,1)} %lat_hbm.1, bf16[32,64]{1,0:T(8,128)(2,1)} %fresh_hbm.1, s32[2]{0:T(128)} %steps_hbm.1, s32[64]{0:T(128)} %slots_hbm.1, s32[64]{0:T(128)} %wins_hbm.1, ...), custom_call_target="tpu_custom_call" | custom-call | flops 4831838208 | bytes 9437184 | tf_op jit(solution)/shard_map/pallas_call | solution.py:570
  80.4 2.0 %shard_map.113 = (bf16[32,2,3072]{2,1,0:T(2,128)(2,1)}, bf16[32,2,64]{2,1,0:T(2,128)(2,1)}, bf16[32,2,64]{2,1,0:T(2,128)(2,1)}) custom-call(bf16[2,32,3072]{2,1,0:T(8,128)(2,1)} %get-tuple-element.6.refs_0_, bf16[2,32,64]{2,1,0:T(8,128)(2,1)} %get-tuple-element.7.refs_1_, bf16[2,32,64]{2,1,0:T(8,128)(2,1)} %get-tuple-element.8.refs_2_), custom_call_target="tpu_custom_call" | custom-call | tf_op jit(solution)/shard_map/pallas_call | solution.py:643

commit v6 on v5

--- a/solution.py
+++ b/solution.py
@@ -58,9 +58,7 @@
     wout_turned,
     mw,
     fw,
-    part,
     mod,
-    gate_part,
     gates_all,
     pattern,
     norm,
@@ -116,7 +114,7 @@
         return copies
 
     barrier = pltpu.get_barrier_semaphore()
-    for k in range(1, Z):
+    for k in (1, 2, Z - 2, Z - 1):
         pl.semaphore_signal(
             barrier, inc=1, device_id=(q, lax.rem(z + k, Z)), device_id_type=MESH
         )
@@ -161,7 +159,7 @@
             part_of = u - 1 if way == 0 else 2 - u
             gather_copy(way, u, hid_hbm.at[pl.ds(part_of * half, half)], z, part_of).start()
 
-    pl.semaphore_wait(barrier, Z + 1)
+    pl.semaphore_wait(barrier, 6)
     own_copies(1)
 
     small[0].wait()
@@ -178,36 +176,40 @@
     rows = lax.broadcasted_iota(jnp.int32, (8, MP), 0)
     pairs = jnp.where(rows < 2, maps[0], maps[1])
     my_columns = pl.ds(pl.multiple_of(z * MP, MP), MP)
-    part[...] = pairs[: 2 * F]
-    gate_part[...] = maps[2][:F]
-
-    def mod_copy(k, owner):
+    mod[:, my_columns] = pairs[: 2 * F]
+    gates_all[:, my_columns] = maps[2][:F]
+
+    def map_copy(i, here, maps_ref, send, recv):
+        distance = (1, Z - 1, 2, Z - 2, 1, 2, Z - 1)[i]
+        origin = (0, 0, 0, 0, Z - 2, Z - 2, 2)[i]
+        owner = lax.rem(z + origin + (0 if here else Z - distance), Z)
+        columns = maps_ref.at[:, pl.ds(pl.multiple_of(owner * MP, MP), MP)]
         return pltpu.make_async_remote_copy(
-            src_ref=part,
-            dst_ref=mod.at[:, pl.ds(pl.multiple_of(owner * MP, MP), MP)],
-            send_sem=mod_send.at[k],
-            recv_sem=mod_recv.at[k],
-            device_id=(q, lax.rem(z + k, Z)),
+            src_ref=columns,
+            dst_ref=columns,
+            send_sem=send.at[i],
+            recv_sem=recv.at[i],
+            device_id=(q, lax.rem(z + distance, Z)),
             device_id_type=MESH,
         )
 
-    def gate_copy(k, owner):
-        return pltpu.make_async_remote_copy(
-            src_ref=gate_part,
-            dst_ref=gates_all.at[:, pl.ds(pl.multiple_of(owner * MP, MP), MP)],
-            send_sem=gate_send.at[k],
-            recv_sem=gate_recv.at[k],
-            device_id=(q, lax.rem(z + k, Z)),
-            device_id_type=MESH,
-        )
-
-    for k in range(1, Z):
-        mod_copy(k, z).start()
+    def mod_copy(i, here=True):
+        return map_copy(i, here, mod, mod_send, mod_recv)
+
+    def gate_copy(i, here=True):
+        return map_copy(i, here, gates_all, gate_send, gate_recv)
+
+    def hand_on(copy):
+        for i in (2, 3):
+            copy(i, False).wait_recv()
+        for i in (4, 5, 6):
+            copy(i).start()
+
+    for i in range(4):
+        mod_copy(i).start()
     own_copies(2)
     for copy in small[1:] + weights + [fw_copy]:
         copy.start()
-    mod[:, my_columns] = part[...]
-    gates_all[:, my_columns] = gate_part[...]
     in_r[0] = jnp.zeros((T, D), BF16)
     in_l[0] = jnp.zeros((T, D), BF16)
 
@@ -239,9 +241,11 @@
         right = (lax.rem(z + step, Z), lax.rem(u, 2))
         return left, right
 
+    hand_on(mod_copy)
     pass_on(1)
-    for k in range(1, Z):
-        mod_copy(k, lax.rem(z + Z - k, Z)).wait_recv()
+    pass_on(2)
+    for i in (0, 1, 4, 5, 6):
+        mod_copy(i, False).wait_recv()
     rows = lax.broadcasted_iota(jnp.int32, (8, D), 0)
     for p in (0, 1):
         pattern[p] = jnp.where(
@@ -305,7 +309,7 @@
 
     def gather_unit(u, carry):
         places = gather_place(u)
-        pl.when(u >= 2)(lambda: pass_on(u))
+        pl.when(u >= 3)(lambda: pass_on(u))
 
         for way in (0, 1):
             normalise(*places[way], way * T)
@@ -329,8 +333,8 @@
         return carry
 
     lax.fori_loop(0, Z, gather_unit, 0)
-    for k in range(1, Z):
-        gate_copy(k, z).start()
+    for i in range(4):
+        gate_copy(i).start()
 
     def spatial(pieces):
         each = [(chunk, frame, h) for chunk, frame in pieces for h in range(LH)]
@@ -480,6 +484,7 @@
 
         @pl.when(m == own_turn)
         def _():
+            hand_on(gate_copy)
             lax.fori_loop(0, Z, drain, 0)
 
         return carry
@@ -488,10 +493,11 @@
 
     lax.fori_loop(1, Z - 2, sent_off, 0)
     fw_copy.wait()
-    for k in range(1, Z):
-        gate_copy(k, lax.rem(z + Z - k, Z)).wait_recv()
-        gate_copy(k, z).wait_send()
-        mod_copy(k, z).wait_send()
+    for i in (0, 1, 4, 5, 6):
+        gate_copy(i, False).wait_recv()
+    for i in range(7):
+        gate_copy(i).wait_send()
+        mod_copy(i).wait_send()
     horizon = STRIDE * (FRAMES + 1)
     LAT = lat.shape[2]
 
@@ -590,9 +596,7 @@
             pltpu.VMEM((W // 4, D), BF16),
             pltpu.VMEM(mod_weight.shape, BF16),
             pltpu.VMEM((LAT, D), BF16),
-            pltpu.VMEM((2 * F, MP), F32),
             pltpu.VMEM((2 * F, D), F32),
-            pltpu.VMEM((F, MP), F32),
             pltpu.VMEM((F, D), F32),
             pltpu.VMEM((2, 8, D), F32),
             pltpu.VMEM((2 * T, D), BF16),

time: 82.5 us -> 82.9 us (level)
  no operation moved by 1% of the time
where the time goes in v6:
time: 82.9 us; the launch traced here: 82.8 us
  Pallas kernels  82.2 us (99%)
    pallas_call x1, Pallas kernels, shards(): pl.pallas_call(functools.partial(kernel, Q, Z), out_shape=(jax.ShapeDtype...  80.2 us
    pallas_call x1, Pallas kernels, shards(): pl.pallas_call(by_token, out_shape=tuple((jax.ShapeDtypeStruct((T, F, x.s...  1.96 us

profile of v6, /device:TPU:1, one launch (start us, length us, event | category | flops | bytes accessed | tf_op | source)
XLA Modules:
  0.0 82.8 jit_solution(13309749767554659535)
XLA Ops:
  0.6 80.2 %shard_map.112 = (bf16[2,32,3072]{2,1,0:T(8,128)(2,1)}, bf16[2,32,64]{2,1,0:T(8,128)(2,1)}, bf16[2,32,64]{2,1,0:T(8,128)(2,1)}) custom-call(bf16[32,2,3072]{2,1,0:T(2,128)(2,1)} %hid_hbm.1, bf16[32,2,64]{2,1,0:T(2,128)(2,1)} %lat_hbm.1, bf16[32,64]{1,0:T(8,128)(2,1)} %fresh_hbm.1, s32[2]{0:T(128)} %steps_hbm.1, s32[64]{0:T(128)} %slots_hbm.1, s32[64]{0:T(128)} %wins_hbm.1, ...), custom_call_target="tpu_custom_call" | custom-call | flops 4831838208 | bytes 9437184 | tf_op jit(solution)/shard_map/pallas_call | solution.py:576
  80.8 2.0 %shard_map.113 = (bf16[32,2,3072]{2,1,0:T(2,128)(2,1)}, bf16[32,2,64]{2,1,0:T(2,128)(2,1)}, bf16[32,2,64]{2,1,0:T(2,128)(2,1)}) custom-call(bf16[2,32,3072]{2,1,0:T(8,128)(2,1)} %get-tuple-element.6.refs_0_, bf16[2,32,64]{2,1,0:T(8,128)(2,1)} %get-tuple-element.7.refs_1_, bf16[2,32,64]{2,1,0:T(8,128)(2,1)} %get-tuple-element.8.refs_2_), custom_call_target="tpu_custom_call" | custom-call | tf_op jit(solution)/shard_map/pallas_call | solution.py:647
